TPU v7x, 128 devices: a whole 4x4x4 slice. The times are simulated.
128 devices in a mesh: group: 4 (over z), dev: 32 (over x, y, core).
Axes of the slice: x: 4, y: 4, z: 4, core: 2. Of those that a mesh axis runs over, the one named last changes fastest.
Arguments:
- populations: float32 [512, 19, 4096], P(('group', 'dev')), may hold values from -3 to 3
- fluid_flags: int32 [512, 4096], P(('group', 'dev')), may hold values from 0 to 1, as said below
- neighbours: int32 [512, 18], P(('group', 'dev')), may hold values from -1 to 11, as said below
- relax_rate: float32 [512], P(('group', 'dev')), may hold values from 1 to 1.9
Outputs:
- advanced: float32 [512, 19, 4096], P(('group', 'dev'))
Inputs may be any that keep to these rules, and one draw needn't show every extreme that they name: `fluid_flags`: on every device the slots that hold a block come first and the later slots have no fluid cell. In every group some device holds a block in all 4 slots. `neighbours`: an entry is -1 or (dz + 1) * 4 + t, where dz is the third component of the direction; it names slot t of the device dz places further along dev in the same group, a slot that holds a block, and that block's entry in the opposite direction names back. Slots that hold no block have -1 in every direction.
All inputs are finite; a program needn't handle non-finite values.
Results may differ from a plain program's by a relative error of at most 0.0003.
Values sent between devices are 32-bit elements; how exact they have to be, the bound alone decides.
A program may use at most 128 MiB of HBM per device.

v0:
```python
import jax
import jax.numpy as jnp
import numpy as np
from jax import lax
from jax.sharding import PartitionSpec as P

BLOCK = 16
STEPS = 2


def extended(x, sides, width):
    for axis, dim in sides:
        peers, length = (lax.axis_size(axis), x.shape[dim])
        up = [(i, (i + 1) % peers) for i in range(peers - 1)]
        down = [(j, i) for i, j in up]
        last = lax.slice_in_dim(x, length - width, length, axis=dim)
        first = lax.slice_in_dim(x, 0, width, axis=dim)
        before = lax.ppermute(last, axis, up)
        after = lax.ppermute(first, axis, down)
        x = jnp.concatenate([before, x, after], axis=dim)
    return x


def invert_matrix(rows_in):
    size_n = len(rows_in)
    work = [
        list(rows_in[row_num]) + [1.0 if col_num == row_num else 0.0 for col_num in range(size_n)]
        for row_num in range(size_n)
    ]
    for col_num in range(size_n):
        pivot_row = max(range(col_num, size_n), key=lambda row_num: abs(work[row_num][col_num]))
        work[col_num], work[pivot_row] = (work[pivot_row], work[col_num])
        pivot_val = work[col_num][col_num]
        work[col_num] = [entry / pivot_val for entry in work[col_num]]
        for row_num in range(size_n):
            if row_num != col_num:
                factor = work[row_num][col_num]
                if factor != 0.0:
                    work[row_num] = [
                        entry - factor * pivot_entry
                        for entry, pivot_entry in zip(work[row_num], work[col_num])
                    ]
    return [row_list[size_n:] for row_list in work]


def lattice():
    velocity = [[0, 0, 0]]
    for axis_num in range(3):
        for side_sign in (1, -1):
            vector = [0, 0, 0]
            vector[axis_num] = side_sign
            velocity.append(vector)
    for axis_one, axis_two in ((0, 1), (0, 2), (1, 2)):
        for sign_one in (1, -1):
            for sign_two in (1, -1):
                vector = [0, 0, 0]
                vector[axis_one] = sign_one
                vector[axis_two] = sign_two
                velocity.append(vector)
    weights = [1.0 / 3.0] + [1.0 / 18.0] * 6 + [1.0 / 36.0] * 12
    opposite = [velocity.index([-entry for entry in velocity[lane_num]]) for lane_num in range(19)]
    comp_x = [float(vector[0]) for vector in velocity]
    comp_y = [float(vector[1]) for vector in velocity]
    comp_z = [float(vector[2]) for vector in velocity]
    makers = [
        lambda a, b, c: 1.0,
        lambda a, b, c: a,
        lambda a, b, c: b,
        lambda a, b, c: c,
        lambda a, b, c: a * b,
        lambda a, b, c: a * c,
        lambda a, b, c: b * c,
        lambda a, b, c: a * a - b * b,
        lambda a, b, c: a * a - c * c,
        lambda a, b, c: a * a + b * b + c * c,
        lambda a, b, c: a * b * b,
        lambda a, b, c: a * c * c,
        lambda a, b, c: b * a * a,
        lambda a, b, c: b * c * c,
        lambda a, b, c: c * a * a,
        lambda a, b, c: c * b * b,
        lambda a, b, c: a * a * b * b,
        lambda a, b, c: a * a * c * c,
        lambda a, b, c: b * b * c * c,
    ]
    moment_rows = [
        [maker(comp_x[col_num], comp_y[col_num], comp_z[col_num]) for col_num in range(19)]
        for maker in makers
    ]
    inverse = invert_matrix(moment_rows)
    table_other = []
    table_shear = []
    for row_num in range(19):
        other_row = []
        shear_row = []
        for col_num in range(19):
            other_sum = sum(
                (
                    inverse[row_num][mom_num] * moment_rows[mom_num][col_num]
                    for mom_num in range(9, 19)
                )
            )
            shear_sum = sum(
                (
                    inverse[row_num][mom_num] * moment_rows[mom_num][col_num]
                    for mom_num in range(4, 9)
                )
            )
            ratio = weights[col_num] / weights[row_num]
            other_row.append(other_sum * ratio)
            shear_row.append(shear_sum * ratio)
        table_other.append(other_row)
        table_shear.append(shear_row)
    return (
        np.array(velocity),
        np.array(weights),
        opposite,
        np.array(table_other),
        np.array(table_shear),
    )


def collide(current, rates):
    velocity, weights, opposite, table_other, table_shear = lattice()
    moment_in = np.concatenate([weights[None, :], (weights[:, None] * velocity).T], 0)
    density_momentum = jnp.einsum(
        "ki,nic->nkc", jnp.asarray(moment_in, jnp.float32), current, precision=lax.Precision.HIGHEST
    )
    density = density_momentum[:, 0]
    momentum = density_momentum[:, 1:]
    projected = jnp.einsum(
        "ik,nkc->nic", jnp.asarray(velocity, jnp.float32), momentum, precision=lax.Precision.HIGHEST
    )
    speed_sq = jnp.sum(momentum * momentum, axis=1)
    equilibrium = (
        density[:, None] + 3.0 * projected + 4.5 * projected * projected - 1.5 * speed_sq[:, None]
    )
    departure = current - equilibrium
    matrices = (
        jnp.asarray(table_other, jnp.float32)[None]
        + rates[:, None, None] * jnp.asarray(table_shear, jnp.float32)[None]
    )
    return current - jnp.einsum(
        "nij,njc->nic", matrices, departure, precision=lax.Precision.HIGHEST
    )


def make_slabs(collided, fluid_flags):
    velocity = lattice()[0]
    block_count = collided.shape[0]
    blocked = collided.reshape(block_count, 19, BLOCK, BLOCK, BLOCK)
    wet_cells = fluid_flags.reshape(block_count, BLOCK, BLOCK, BLOCK).astype(jnp.float32)
    face_list = []
    for lane_num in range(1, 7):
        axis_num = int(np.argmax(np.abs(velocity[lane_num])))
        side_sign = int(velocity[lane_num][axis_num])
        layer_index = BLOCK - 1 if side_sign > 0 else 0
        members = [
            lane_two for lane_two in range(19) if int(velocity[lane_two][axis_num]) == side_sign
        ]
        layer_values = lax.index_in_dim(blocked, layer_index, axis_num + 2, keepdims=False)[
            :, members
        ]
        layer_flags = lax.index_in_dim(wet_cells, layer_index, axis_num + 1, keepdims=False)
        face_list.append(
            jnp.concatenate([layer_values, layer_flags[:, None]], 1).reshape(
                block_count, 6, BLOCK * BLOCK
            )
        )
    edge_list = []
    for lane_num in range(7, 19):
        nonzero = [axis_num for axis_num in range(3) if int(velocity[lane_num][axis_num]) != 0]
        axis_one, axis_two = nonzero
        end_one = BLOCK - 1 if velocity[lane_num][axis_one] > 0 else 0
        end_two = BLOCK - 1 if velocity[lane_num][axis_two] > 0 else 0
        line_values = lax.index_in_dim(
            lax.index_in_dim(blocked[:, lane_num], end_one, axis_one + 1, keepdims=False),
            end_two,
            axis_two,
            keepdims=False,
        )
        line_flags = lax.index_in_dim(
            lax.index_in_dim(wet_cells, end_one, axis_one + 1, keepdims=False),
            end_two,
            axis_two,
            keepdims=False,
        )
        edge_list.append(jnp.stack([line_values, line_flags], 1))
    return (jnp.stack(face_list, 1), jnp.stack(edge_list, 1))


def propagate(current, collided, fluid_flags, rim_faces, rim_edges):
    velocity, weights, opposite, table_other, table_shear = lattice()
    block_count = current.shape[0]
    blocked = collided.reshape(block_count, 19, BLOCK, BLOCK, BLOCK)
    wet_cells = fluid_flags.reshape(block_count, BLOCK, BLOCK, BLOCK).astype(jnp.float32)
    padded = jnp.zeros((block_count, 19, BLOCK + 2, BLOCK + 2, BLOCK + 2), collided.dtype)
    padded = padded.at[:, :, 1:-1, 1:-1, 1:-1].set(blocked)
    open_mask = jnp.zeros((block_count, BLOCK + 2, BLOCK + 2, BLOCK + 2), wet_cells.dtype)
    open_mask = open_mask.at[:, 1:-1, 1:-1, 1:-1].set(wet_cells)
    inner = slice(1, BLOCK + 1)
    for face_num in range(6):
        lane_num = face_num + 1
        axis_num = int(np.argmax(np.abs(velocity[lane_num])))
        side_sign = int(velocity[lane_num][axis_num])
        rim_at = BLOCK + 1 if side_sign > 0 else 0
        spatial = tuple((rim_at if axis_two == axis_num else inner for axis_two in range(3)))
        members = [
            lane_two for lane_two in range(19) if int(velocity[lane_two][axis_num]) == -side_sign
        ]
        face_values = rim_faces[:, face_num].reshape(block_count, 6, BLOCK, BLOCK)
        for member_num, lane_two in enumerate(members):
            padded = padded.at[(slice(None), lane_two) + spatial].set(face_values[:, member_num])
        open_mask = open_mask.at[(slice(None),) + spatial].set(face_values[:, 5])
    for edge_num in range(12):
        lane_num = edge_num + 7
        spatial = tuple(
            (
                (
                    (BLOCK + 1 if velocity[lane_num][axis_two] > 0 else 0)
                    if int(velocity[lane_num][axis_two]) != 0
                    else inner
                )
                for axis_two in range(3)
            )
        )
        padded = padded.at[(slice(None), opposite[lane_num]) + spatial].set(
            rim_edges[:, edge_num, 0]
        )
        open_mask = open_mask.at[(slice(None),) + spatial].set(rim_edges[:, edge_num, 1])
    arrived_list = []
    for lane_num in range(19):
        window = tuple(
            (
                slice(1 - int(component), 1 - int(component) + BLOCK)
                for component in velocity[lane_num]
            )
        )
        pulled = padded[(slice(None), lane_num) + window]
        open_here = open_mask[(slice(None),) + window]
        arrived_list.append(jnp.where(open_here > 0, pulled, blocked[:, opposite[lane_num]]))
    arrived = jnp.stack(arrived_list, 1).reshape(block_count, 19, BLOCK * BLOCK * BLOCK)
    return jnp.where(fluid_flags[:, None, :] > 0, arrived, current)


def live_slots(fluid_flags):
    holds = jnp.max(fluid_flags, axis=1) > 0
    ranks = jnp.arange(1, fluid_flags.shape[0] + 1, dtype=jnp.int32)
    return jnp.max(jnp.where(holds, ranks, 0)).astype(jnp.int32)


def collide_live(current, rates, fluid_flags, occupied):
    slot_count = current.shape[0]
    batch_size = min(8, slot_count)
    turn_count = (occupied + batch_size - 1) // batch_size
    face_init = jnp.zeros((slot_count, 6, 6, BLOCK * BLOCK), jnp.float32)
    edge_init = jnp.zeros((slot_count, 12, 2, BLOCK), jnp.float32)

    def collide_one_turn(turn_num, carried):
        collided_all, face_all, edge_all = carried
        first_slot = turn_num * batch_size
        part_now = lax.dynamic_slice_in_dim(current, first_slot, batch_size, 0)
        rates_now = lax.dynamic_slice_in_dim(rates, first_slot, batch_size, 0)
        flags_now = lax.dynamic_slice_in_dim(fluid_flags, first_slot, batch_size, 0)
        collided = collide(part_now, rates_now)
        face_part, edge_part = make_slabs(collided, flags_now)
        return (
            lax.dynamic_update_slice_in_dim(collided_all, collided, first_slot, 0),
            lax.dynamic_update_slice_in_dim(face_all, face_part, first_slot, 0),
            lax.dynamic_update_slice_in_dim(edge_all, edge_part, first_slot, 0),
        )

    return lax.fori_loop(
        0, turn_count, collide_one_turn, (jnp.zeros_like(current), face_init, edge_init)
    )


def propagate_live(current, collided_all, fluid_flags, rim_faces, rim_edges, occupied):
    slot_count = current.shape[0]
    batch_size = min(8, slot_count)
    turn_count = (occupied + batch_size - 1) // batch_size

    def propagate_one_turn(turn_num, carried):
        first_slot = turn_num * batch_size
        part_now = lax.dynamic_slice_in_dim(carried, first_slot, batch_size, 0)
        collided = lax.dynamic_slice_in_dim(collided_all, first_slot, batch_size, 0)
        flags_now = lax.dynamic_slice_in_dim(fluid_flags, first_slot, batch_size, 0)
        faces_now = lax.dynamic_slice_in_dim(rim_faces, first_slot, batch_size, 0)
        edges_now = lax.dynamic_slice_in_dim(rim_edges, first_slot, batch_size, 0)
        updated = propagate(part_now, collided, flags_now, faces_now, edges_now)
        return lax.dynamic_update_slice_in_dim(carried, updated, first_slot, 0)

    return lax.fori_loop(0, turn_count, propagate_one_turn, current)


def gather_rims(face_slabs, edge_slabs, neighbours):
    slot_count = face_slabs.shape[0]
    face_len = 6 * BLOCK * BLOCK
    upper_edges = [4, 6, 8, 10]
    lower_edges = [5, 7, 9, 11]
    upward = jnp.concatenate(
        [
            face_slabs[:, 4].reshape(slot_count, -1),
            edge_slabs[:, upper_edges].reshape(slot_count, -1),
        ],
        1,
    )
    downward = jnp.concatenate(
        [
            face_slabs[:, 5].reshape(slot_count, -1),
            edge_slabs[:, lower_edges].reshape(slot_count, -1),
        ],
        1,
    )
    stacked = jnp.stack([downward, upward], 0)
    widened = extended(stacked, (("dev", 0),), 1)
    from_below = widened[0]
    from_above = widened[3]
    below_faces = from_below[:, :face_len].reshape(slot_count, 6, BLOCK * BLOCK)
    below_edges = from_below[:, face_len:].reshape(slot_count, 4, 2, BLOCK)
    above_faces = from_above[:, :face_len].reshape(slot_count, 6, BLOCK * BLOCK)
    above_edges = from_above[:, face_len:].reshape(slot_count, 4, 2, BLOCK)
    present = neighbours >= 0
    target = jnp.where(present, neighbours % slot_count, 0)
    face_list = []
    for face_num in range(6):
        if face_num < 4:
            source = face_slabs[:, face_num ^ 1]
        elif face_num == 4:
            source = above_faces
        else:
            source = below_faces
        face_list.append(
            jnp.where(present[:, face_num, None, None], source[target[:, face_num]], 0.0)
        )
    edge_list = []
    for edge_num in range(12):
        column = 6 + edge_num
        opposite_edge = 4 * (edge_num // 4) + 3 - edge_num % 4
        if edge_num < 4:
            source = edge_slabs[:, opposite_edge]
        elif edge_num % 2 == 0:
            source = above_edges[:, lower_edges.index(opposite_edge)]
        else:
            source = below_edges[:, upper_edges.index(opposite_edge)]
        edge_list.append(jnp.where(present[:, column, None, None], source[target[:, column]], 0.0))
    return (jnp.stack(face_list, 1), jnp.stack(edge_list, 1))


def body(populations, fluid_flags, neighbours, relax_rate):
    live_count = live_slots(fluid_flags)
    current = populations
    for step_num in range(STEPS):
        collided, face_slabs, edge_slabs = collide_live(
            current, relax_rate, fluid_flags, live_count
        )
        rim_faces, rim_edges = gather_rims(face_slabs, edge_slabs, neighbours)
        current = propagate_live(current, collided, fluid_flags, rim_faces, rim_edges, live_count)
    return current


def solution(mesh):
    placed = (
        P(("group", "dev"), None, None),
        P(("group", "dev"), None),
        P(("group", "dev"), None),
        P(("group", "dev")),
    )
    return jax.shard_map(
        body, mesh=mesh, in_specs=placed, out_specs=P(("group", "dev"), None, None), check_vma=False
    )
```

profile of v0, /device:TPU:38, one launch (start us, length us, event | category | flops | bytes accessed | tf_op | source)
XLA Modules:
  0.0 1037.2 jit_solution(4772186889672003397)
XLA Ops:
  140.1 385.0 %while.191 = (s32[]{:T(128)}, f32[4,19,4096]{2,0,1:T(4,128)S(1)}, s32[]{:T(128)}, s32[4,4096]{1,0:T(4,128)S(1)}, f32[4,16,16,16]{3,2,1,0:T(8,128)S(1)}, /*index=...) while((s32[]{:T(128)}, f32[4,19,4096]{2,0,1:T(4,128)S(1)}, ...), condition=%wide.region_6.7_spmd, body=%wide.region_5.6_spmd.sunk | while | flops 950274 | bytes 42097896 | solution.py:293
  149.0 11.6 %scatter.744 = f32[4,19,18,18,18]{4,3,2,0,1:T(8,128)} pad(f32[4,19,16,16,16]{4,3,2,0,1:T(8,128)} %reshape.7441, f32[]{:T(128)} %constant.5125.clone.1..sunk), padding=0_0x0_0x1_1x1_1x1_1 | pad | bytes 3018116 | tf_op jit(solution)/shard_map/while/body/scatter | solution.py:198
  188.1 10.4 %scatter.755 = f32[4,19,18,18,18]{4,3,2,0,1:T(8,128)} dynamic-update-slice(f32[4,19,18,18,18]{4,3,2,0,1:T(8,128)} %scatter.754, f32[4,1,16,1,16]{4,3,2,0,1:T(1,128)S(1)} %bitcast.1388, s32[]{:T(128)} %constant.5119.clone.1..sunk, s32[]{:T(128)} %constant.5091.clone.1..sunk, s32[]{:T(128)} %constant.5121.clone.1..sunk.1, s32[]{:T(128)} %constant.5081.clone.1..sunk, s32[]{:T(128)} %constant.5121.clone.1..sunk.1) | dynamic-update-slice | bytes 8196 | tf_op jit(solution)/shard_map/while/body/scatter | solution.py:213
  198.5 10.4 %scatter.756 = f32[4,19,18,18,18]{4,3,2,0,1:T(8,128)} dynamic-update-slice(f32[4,19,18,18,18]{4,3,2,0,1:T(8,128)} %scatter.755, f32[4,1,16,1,16]{4,3,2,0,1:T(1,128)S(1)} %bitcast.1384, s32[]{:T(128)} %constant.5119.clone.1..sunk, s32[]{:T(128)} %constant.5088.clone.1..sunk, s32[]{:T(128)} %constant.5121.clone.1..sunk.1, s32[]{:T(128)} %constant.5081.clone.1..sunk, s32[]{:T(128)} %constant.5121.clone.1..sunk.1) | dynamic-update-slice | bytes 8196 | tf_op jit(solution)/shard_map/while/body/scatter | solution.py:213
  209.0 10.4 %scatter.757 = f32[4,19,18,18,18]{4,3,2,0,1:T(8,128)} dynamic-update-slice(f32[4,19,18,18,18]{4,3,2,0,1:T(8,128)} %scatter.756, f32[4,1,16,1,16]{4,3,2,0,1:T(1,128)S(1)} %bitcast.1380, s32[]{:T(128)} %constant.5119.clone.1..sunk, s32[]{:T(128)} %constant.5084.clone.1..sunk, s32[]{:T(128)} %constant.5121.clone.1..sunk.1, s32[]{:T(128)} %constant.5081.clone.1..sunk, s32[]{:T(128)} %constant.5121.clone.1..sunk.1) | dynamic-update-slice | bytes 8196 | tf_op jit(solution)/shard_map/while/body/scatter | solution.py:213
  219.4 10.4 %scatter.758 = f32[4,19,18,18,18]{4,3,2,0,1:T(8,128)} dynamic-update-slice(f32[4,19,18,18,18]{4,3,2,0,1:T(8,128)} %scatter.757, f32[4,1,16,1,16]{4,3,2,0,1:T(1,128)S(1)} %bitcast.1376, s32[]{:T(128)} %constant.5119.clone.1..sunk, s32[]{:T(128)} %constant.5081.clone.1..sunk, s32[]{:T(128)} %constant.5121.clone.1..sunk.1, s32[]{:T(128)} %constant.5081.clone.1..sunk, s32[]{:T(128)} %constant.5121.clone.1..sunk.1) | dynamic-update-slice | bytes 8196 | tf_op jit(solution)/shard_map/while/body/scatter | solution.py:213
  229.9 10.4 %scatter.759 = f32[4,19,18,18,18]{4,3,2,0,1:T(8,128)} dynamic-update-slice(f32[4,19,18,18,18]{4,3,2,0,1:T(8,128)} %scatter.758, f32[4,1,16,1,16]{4,3,2,0,1:T(1,128)S(1)} %bitcast.1372, s32[]{:T(128)} %constant.5119.clone.1..sunk, s32[]{:T(128)} %constant.5092.clone.1..sunk, s32[]{:T(128)} %constant.5121.clone.1..sunk.1, s32[]{:T(128)} %constant.5081.clone.1..sunk, s32[]{:T(128)} %constant.5121.clone.1..sunk.1) | dynamic-update-slice | bytes 8196 | tf_op jit(solution)/shard_map/while/body/scatter | solution.py:213
  240.5 10.4 %scatter.760 = f32[4,19,18,18,18]{4,3,2,0,1:T(8,128)} dynamic-update-slice(f32[4,19,18,18,18]{4,3,2,0,1:T(8,128)} %scatter.759, f32[4,1,16,1,16]{4,3,2,0,1:T(1,128)S(1)} %bitcast.1389, s32[]{:T(128)} %constant.5119.clone.1..sunk, s32[]{:T(128)} %constant.5122.clone.1..sunk, s32[]{:T(128)} %constant.5121.clone.1..sunk.1, s32[]{:T(128)} %constant.5119.clone.1..sunk, s32[]{:T(128)} %constant.5121.clone.1..sunk.1) | dynamic-update-slice | bytes 8196 | tf_op jit(solution)/shard_map/while/body/scatter | solution.py:213
  250.9 10.4 %scatter.761 = f32[4,19,18,18,18]{4,3,2,0,1:T(8,128)} dynamic-update-slice(f32[4,19,18,18,18]{4,3,2,0,1:T(8,128)} %scatter.760, f32[4,1,16,1,16]{4,3,2,0,1:T(1,128)S(1)} %bitcast.1385, s32[]{:T(128)} %constant.5119.clone.1..sunk, s32[]{:T(128)} %constant.5087.clone.1..sunk, s32[]{:T(128)} %constant.5121.clone.1..sunk.1, s32[]{:T(128)} %constant.5119.clone.1..sunk, s32[]{:T(128)} %constant.5121.clone.1..sunk.1) | dynamic-update-slice | bytes 8196 | tf_op jit(solution)/shard_map/while/body/scatter | solution.py:213
  261.4 10.4 %scatter.762 = f32[4,19,18,18,18]{4,3,2,0,1:T(8,128)} dynamic-update-slice(f32[4,19,18,18,18]{4,3,2,0,1:T(8,128)} %scatter.761, f32[4,1,16,1,16]{4,3,2,0,1:T(1,128)S(1)} %bitcast.1381, s32[]{:T(128)} %constant.5119.clone.1..sunk, s32[]{:T(128)} %constant.5083.clone.1..sunk, s32[]{:T(128)} %constant.5121.clone.1..sunk.1, s32[]{:T(128)} %constant.5119.clone.1..sunk, s32[]{:T(128)} %constant.5121.clone.1..sunk.1) | dynamic-update-slice | bytes 8196 | tf_op jit(solution)/shard_map/while/body/scatter | solution.py:213
  271.8 10.4 %scatter.763 = f32[4,19,18,18,18]{4,3,2,0,1:T(8,128)} dynamic-update-slice(f32[4,19,18,18,18]{4,3,2,0,1:T(8,128)} %scatter.762, f32[4,1,16,1,16]{4,3,2,0,1:T(1,128)S(1)} %bitcast.1377, s32[]{:T(128)} %constant.5119.clone.1..sunk, s32[]{:T(128)} %constant.5094.clone.1..sunk, s32[]{:T(128)} %constant.5121.clone.1..sunk.1, s32[]{:T(128)} %constant.5119.clone.1..sunk, s32[]{:T(128)} %constant.5121.clone.1..sunk.1) | dynamic-update-slice | bytes 8196 | tf_op jit(solution)/shard_map/while/body/scatter | solution.py:213
  282.3 10.4 %scatter.764 = f32[4,19,18,18,18]{4,3,2,0,1:T(8,128)} dynamic-update-slice(f32[4,19,18,18,18]{4,3,2,0,1:T(8,128)} %scatter.763, f32[4,1,16,1,16]{4,3,2,0,1:T(1,128)S(1)} %bitcast.1373, s32[]{:T(128)} %constant.5119.clone.1..sunk, s32[]{:T(128)} %constant.5095.clone.1..sunk, s32[]{:T(128)} %constant.5121.clone.1..sunk.1, s32[]{:T(128)} %constant.5119.clone.1..sunk, s32[]{:T(128)} %constant.5121.clone.1..sunk.1) | dynamic-update-slice | bytes 8196 | tf_op jit(solution)/shard_map/while/body/scatter | solution.py:213
  293.3 12.7 %scatter.765 = f32[4,19,18,18,18]{4,3,2,0,1:T(8,128)} dynamic-update-slice(f32[4,19,18,18,18]{4,3,2,0,1:T(8,128)} %scatter.764, f32[4,1,16,16,1]{4,3,2,0,1:T(8,128)S(1)} %copy.753, s32[]{:T(128)} %constant.5119.clone.1..sunk, s32[]{:T(128)} %constant.5096.clone.1..sunk, s32[]{:T(128)} %constant.5121.clone.1..sunk.1, s32[]{:T(128)} %constant.5121.clone.1..sunk.1, s32[]{:T(128)} %constant.5081.clone.1..sunk) | dynamic-update-slice | bytes 8196 | tf_op jit(solution)/shard_map/while/body/scatter | solution.py:213
  306.5 12.5 %scatter.766 = f32[4,19,18,18,18]{4,3,2,0,1:T(8,128)} dynamic-update-slice(f32[4,19,18,18,18]{4,3,2,0,1:T(8,128)} %scatter.765, f32[4,1,16,16,1]{4,3,2,0,1:T(8,128)S(1)} %copy.754, s32[]{:T(128)} %constant.5119.clone.1..sunk, s32[]{:T(128)} %constant.5090.clone.1..sunk, s32[]{:T(128)} %constant.5121.clone.1..sunk.1, s32[]{:T(128)} %constant.5121.clone.1..sunk.1, s32[]{:T(128)} %constant.5081.clone.1..sunk) | dynamic-update-slice | bytes 8196 | tf_op jit(solution)/shard_map/while/body/scatter | solution.py:213
  319.5 12.5 %scatter.767 = f32[4,19,18,18,18]{4,3,2,0,1:T(8,128)} dynamic-update-slice(f32[4,19,18,18,18]{4,3,2,0,1:T(8,128)} %scatter.766, f32[4,1,16,16,1]{4,3,2,0,1:T(8,128)S(1)} %copy.755, s32[]{:T(128)} %constant.5119.clone.1..sunk, s32[]{:T(128)} %constant.5086.clone.1..sunk, s32[]{:T(128)} %constant.5121.clone.1..sunk.1, s32[]{:T(128)} %constant.5121.clone.1..sunk.1, s32[]{:T(128)} %constant.5081.clone.1..sunk) | dynamic-update-slice | bytes 8196 | tf_op jit(solution)/shard_map/while/body/scatter | solution.py:213
  332.5 12.5 %scatter.768 = f32[4,19,18,18,18]{4,3,2,0,1:T(8,128)} dynamic-update-slice(f32[4,19,18,18,18]{4,3,2,0,1:T(8,128)} %scatter.767, f32[4,1,16,16,1]{4,3,2,0,1:T(8,128)S(1)} %copy.756, s32[]{:T(128)} %constant.5119.clone.1..sunk, s32[]{:T(128)} %constant.5095.clone.1..sunk, s32[]{:T(128)} %constant.5121.clone.1..sunk.1, s32[]{:T(128)} %constant.5121.clone.1..sunk.1, s32[]{:T(128)} %constant.5081.clone.1..sunk) | dynamic-update-slice | bytes 8196 | tf_op jit(solution)/shard_map/while/body/scatter | solution.py:213
  345.4 12.5 %scatter.769 = f32[4,19,18,18,18]{4,3,2,0,1:T(8,128)} dynamic-update-slice(f32[4,19,18,18,18]{4,3,2,0,1:T(8,128)} %scatter.768, f32[4,1,16,16,1]{4,3,2,0,1:T(8,128)S(1)} %copy.757, s32[]{:T(128)} %constant.5119.clone.1..sunk, s32[]{:T(128)} %constant.5092.clone.1..sunk, s32[]{:T(128)} %constant.5121.clone.1..sunk.1, s32[]{:T(128)} %constant.5121.clone.1..sunk.1, s32[]{:T(128)} %constant.5081.clone.1..sunk) | dynamic-update-slice | bytes 8196 | tf_op jit(solution)/shard_map/while/body/scatter | solution.py:213
  435.2 11.2 %scatter.792 = f32[4,18,18,18]{3,2,1,0:T(8,128)S(1)} dynamic-update-slice(f32[4,18,18,18]{3,2,1,0:T(8,128)S(1)} %scatter.791, f32[4,16,16,1]{3,2,1,0:T(8,128)S(1)} %copy.771, s32[]{:T(128)} %constant.5119.clone.1..sunk, s32[]{:T(128)} %constant.5121.clone.1..sunk.1, s32[]{:T(128)} %constant.5121.clone.1..sunk.1, s32[]{:T(128)} %constant.5081.clone.1..sunk) | dynamic-update-slice | bytes 8196 | tf_op jit(solution)/shard_map/while/body/scatter | solution.py:214
  655.4 380.4 %while.193 = (s32[]{:T(128)}, f32[4,19,4096]{2,0,1:T(4,128)S(1)}, s32[]{:T(128)}, s32[4,4096]{1,0:T(4,128)S(1)}, f32[4,16,16,16]{3,2,1,0:T(8,128)S(1)}, /*index=...) while((s32[]{:T(128)}, f32[4,19,4096]{2,0,1:T(4,128)S(1)}, ...), condition=%wide.region_11.12_spmd, body=%wide.region_10.11_spmd.sunk | while | flops 950274 | bytes 42097896 | solution.py:293
  664.2 11.6 %scatter.806 = f32[4,19,18,18,18]{4,3,2,0,1:T(8,128)} pad(f32[4,19,16,16,16]{4,3,2,0,1:T(8,128)} %reshape.7442, f32[]{:T(128)} %constant.5125.clone.1..sunk.1), padding=0_0x0_0x1_1x1_1x1_1 | pad | bytes 3018116 | tf_op jit(solution)/shard_map/while/body/scatter | solution.py:198
  703.3 10.4 %scatter.817 = f32[4,19,18,18,18]{4,3,2,0,1:T(8,128)} dynamic-update-slice(f32[4,19,18,18,18]{4,3,2,0,1:T(8,128)} %scatter.816, f32[4,1,16,1,16]{4,3,2,0,1:T(1,128)S(1)} %bitcast.1390, s32[]{:T(128)} %constant.5119.clone.1..sunk.1, s32[]{:T(128)} %constant.5091.clone.1..sunk.1, s32[]{:T(128)} %constant.5121.clone.1..sunk.3, s32[]{:T(128)} %constant.5081.clone.1..sunk.1, s32[]{:T(128)} %constant.5121.clone.1..sunk.3) | dynamic-update-slice | bytes 8196 | tf_op jit(solution)/shard_map/while/body/scatter | solution.py:213
  713.8 10.4 %scatter.818 = f32[4,19,18,18,18]{4,3,2,0,1:T(8,128)} dynamic-update-slice(f32[4,19,18,18,18]{4,3,2,0,1:T(8,128)} %scatter.817, f32[4,1,16,1,16]{4,3,2,0,1:T(1,128)S(1)} %bitcast.1386, s32[]{:T(128)} %constant.5119.clone.1..sunk.1, s32[]{:T(128)} %constant.5088.clone.1..sunk.1, s32[]{:T(128)} %constant.5121.clone.1..sunk.3, s32[]{:T(128)} %constant.5081.clone.1..sunk.1, s32[]{:T(128)} %constant.5121.clone.1..sunk.3) | dynamic-update-slice | bytes 8196 | tf_op jit(solution)/shard_map/while/body/scatter | solution.py:213
  745.1 10.4 %scatter.821 = f32[4,19,18,18,18]{4,3,2,0,1:T(8,128)} dynamic-update-slice(f32[4,19,18,18,18]{4,3,2,0,1:T(8,128)} %scatter.820, f32[4,1,16,1,16]{4,3,2,0,1:T(1,128)S(1)} %bitcast.1374, s32[]{:T(128)} %constant.5119.clone.1..sunk.1, s32[]{:T(128)} %constant.5092.clone.1..sunk.1, s32[]{:T(128)} %constant.5121.clone.1..sunk.3, s32[]{:T(128)} %constant.5081.clone.1..sunk.1, s32[]{:T(128)} %constant.5121.clone.1..sunk.3) | dynamic-update-slice | bytes 8196 | tf_op jit(solution)/shard_map/while/body/scatter | solution.py:213
  755.7 10.4 %scatter.822 = f32[4,19,18,18,18]{4,3,2,0,1:T(8,128)} dynamic-update-slice(f32[4,19,18,18,18]{4,3,2,0,1:T(8,128)} %scatter.821, f32[4,1,16,1,16]{4,3,2,0,1:T(1,128)S(1)} %bitcast.1391, s32[]{:T(128)} %constant.5119.clone.1..sunk.1, s32[]{:T(128)} %constant.5122.clone.1..sunk.1, s32[]{:T(128)} %constant.5121.clone.1..sunk.3, s32[]{:T(128)} %constant.5119.clone.1..sunk.1, s32[]{:T(128)} %constant.5121.clone.1..sunk.3) | dynamic-update-slice | bytes 8196 | tf_op jit(solution)/shard_map/while/body/scatter | solution.py:213
  776.6 10.4 %scatter.824 = f32[4,19,18,18,18]{4,3,2,0,1:T(8,128)} dynamic-update-slice(f32[4,19,18,18,18]{4,3,2,0,1:T(8,128)} %scatter.823, f32[4,1,16,1,16]{4,3,2,0,1:T(1,128)S(1)} %bitcast.1383, s32[]{:T(128)} %constant.5119.clone.1..sunk.1, s32[]{:T(128)} %constant.5083.clone.1..sunk.1, s32[]{:T(128)} %constant.5121.clone.1..sunk.3, s32[]{:T(128)} %constant.5119.clone.1..sunk.1, s32[]{:T(128)} %constant.5121.clone.1..sunk.3) | dynamic-update-slice | bytes 8196 | tf_op jit(solution)/shard_map/while/body/scatter | solution.py:213
  787.1 10.4 %scatter.825 = f32[4,19,18,18,18]{4,3,2,0,1:T(8,128)} dynamic-update-slice(f32[4,19,18,18,18]{4,3,2,0,1:T(8,128)} %scatter.824, f32[4,1,16,1,16]{4,3,2,0,1:T(1,128)S(1)} %bitcast.1379, s32[]{:T(128)} %constant.5119.clone.1..sunk.1, s32[]{:T(128)} %constant.5094.clone.1..sunk.1, s32[]{:T(128)} %constant.5121.clone.1..sunk.3, s32[]{:T(128)} %constant.5119.clone.1..sunk.1, s32[]{:T(128)} %constant.5121.clone.1..sunk.3) | dynamic-update-slice | bytes 8196 | tf_op jit(solution)/shard_map/while/body/scatter | solution.py:213
  808.6 12.7 %scatter.827 = f32[4,19,18,18,18]{4,3,2,0,1:T(8,128)} dynamic-update-slice(f32[4,19,18,18,18]{4,3,2,0,1:T(8,128)} %scatter.826, f32[4,1,16,16,1]{4,3,2,0,1:T(8,128)S(1)} %copy.781, s32[]{:T(128)} %constant.5119.clone.1..sunk.1, s32[]{:T(128)} %constant.5096.clone.1..sunk.1, s32[]{:T(128)} %constant.5121.clone.1..sunk.3, s32[]{:T(128)} %constant.5121.clone.1..sunk.3, s32[]{:T(128)} %constant.5081.clone.1..sunk.1) | dynamic-update-slice | bytes 8196 | tf_op jit(solution)/shard_map/while/body/scatter | solution.py:213
  821.7 12.5 %scatter.828 = f32[4,19,18,18,18]{4,3,2,0,1:T(8,128)} dynamic-update-slice(f32[4,19,18,18,18]{4,3,2,0,1:T(8,128)} %scatter.827, f32[4,1,16,16,1]{4,3,2,0,1:T(8,128)S(1)} %copy.782, s32[]{:T(128)} %constant.5119.clone.1..sunk.1, s32[]{:T(128)} %constant.5090.clone.1..sunk.1, s32[]{:T(128)} %constant.5121.clone.1..sunk.3, s32[]{:T(128)} %constant.5121.clone.1..sunk.3, s32[]{:T(128)} %constant.5081.clone.1..sunk.1) | dynamic-update-slice | bytes 8196 | tf_op jit(solution)/shard_map/while/body/scatter | solution.py:213
  834.7 12.5 %scatter.829 = f32[4,19,18,18,18]{4,3,2,0,1:T(8,128)} dynamic-update-slice(f32[4,19,18,18,18]{4,3,2,0,1:T(8,128)} %scatter.828, f32[4,1,16,16,1]{4,3,2,0,1:T(8,128)S(1)} %copy.783, s32[]{:T(128)} %constant.5119.clone.1..sunk.1, s32[]{:T(128)} %constant.5086.clone.1..sunk.1, s32[]{:T(128)} %constant.5121.clone.1..sunk.3, s32[]{:T(128)} %constant.5121.clone.1..sunk.3, s32[]{:T(128)} %constant.5081.clone.1..sunk.1) | dynamic-update-slice | bytes 8196 | tf_op jit(solution)/shard_map/while/body/scatter | solution.py:213
  847.7 12.5 %scatter.830 = f32[4,19,18,18,18]{4,3,2,0,1:T(8,128)} dynamic-update-slice(f32[4,19,18,18,18]{4,3,2,0,1:T(8,128)} %scatter.829, f32[4,1,16,16,1]{4,3,2,0,1:T(8,128)S(1)} %copy.784, s32[]{:T(128)} %constant.5119.clone.1..sunk.1, s32[]{:T(128)} %constant.5095.clone.1..sunk.1, s32[]{:T(128)} %constant.5121.clone.1..sunk.3, s32[]{:T(128)} %constant.5121.clone.1..sunk.3, s32[]{:T(128)} %constant.5081.clone.1..sunk.1) | dynamic-update-slice | bytes 8196 | tf_op jit(solution)/shard_map/while/body/scatter | solution.py:213
  860.6 12.5 %scatter.831 = f32[4,19,18,18,18]{4,3,2,0,1:T(8,128)} dynamic-update-slice(f32[4,19,18,18,18]{4,3,2,0,1:T(8,128)} %scatter.830, f32[4,1,16,16,1]{4,3,2,0,1:T(8,128)S(1)} %copy.785, s32[]{:T(128)} %constant.5119.clone.1..sunk.1, s32[]{:T(128)} %constant.5092.clone.1..sunk.1, s32[]{:T(128)} %constant.5121.clone.1..sunk.3, s32[]{:T(128)} %constant.5121.clone.1..sunk.3, s32[]{:T(128)} %constant.5081.clone.1..sunk.1) | dynamic-update-slice | bytes 8196 | tf_op jit(solution)/shard_map/while/body/scatter | solution.py:213
  950.4 11.2 %scatter.854 = f32[4,18,18,18]{3,2,1,0:T(8,128)S(1)} dynamic-update-slice(f32[4,18,18,18]{3,2,1,0:T(8,128)S(1)} %scatter.853, f32[4,16,16,1]{3,2,1,0:T(8,128)S(1)} %copy.799, s32[]{:T(128)} %constant.5119.clone.1..sunk.1, s32[]{:T(128)} %constant.5121.clone.1..sunk.3, s32[]{:T(128)} %constant.5121.clone.1..sunk.3, s32[]{:T(128)} %constant.5081.clone.1..sunk.1) | dynamic-update-slice | bytes 8196 | tf_op jit(solution)/shard_map/while/body/scatter | solution.py:214
  (914 shorter events, 690.0 us)
Async XLA Ops:
  4.2 48.0 %copy-start.64 = (f32[4,1,16]{2,1,0:T(1,128)}, f32[4,1,16]{2,1,0:T(1,128)S(1)}, u32[]{:S(2)}) copy-start(f32[4,1,16]{2,1,0:T(1,128)S(1)} %get-tuple-element.3506) | copy-start | bytes 772
  4.2 48.0 %copy-start.60 = (f32[4,1,16]{2,1,0:T(1,128)}, f32[4,1,16]{2,1,0:T(1,128)S(1)}, u32[]{:S(2)}) copy-start(f32[4,1,16]{2,1,0:T(1,128)S(1)} %get-tuple-element.3505) | copy-start | bytes 772
  4.4 47.8 %copy-start.42 = (f32[4,16]{1,0:T(4,128)}, f32[4,16]{1,0:T(4,128)S(1)}, u32[]{:S(2)}) copy-start(f32[4,16]{1,0:T(4,128)S(1)} %get-tuple-element.3170) | copy-start | bytes 772
  4.4 47.9 %copy-start.44 = (f32[4,16]{1,0:T(4,128)}, f32[4,16]{1,0:T(4,128)S(1)}, u32[]{:S(2)}) copy-start(f32[4,16]{1,0:T(4,128)S(1)} %get-tuple-element.3169) | copy-start | bytes 772
  4.4 47.8 %copy-start.62 = (f32[4,1,16]{2,1,0:T(1,128)}, f32[4,1,16]{2,1,0:T(1,128)S(1)}, u32[]{:S(2)}) copy-start(f32[4,1,16]{2,1,0:T(1,128)S(1)} %get-tuple-element.3504) | copy-start | bytes 772
  4.4 47.9 %copy-start.58 = (f32[4,1,16]{2,1,0:T(1,128)}, f32[4,1,16]{2,1,0:T(1,128)S(1)}, u32[]{:S(2)}) copy-start(f32[4,1,16]{2,1,0:T(1,128)S(1)} %get-tuple-element.3503) | copy-start | bytes 772
  4.6 47.8 %copy-start.46 = (f32[4,16]{1,0:T(4,128)}, f32[4,16]{1,0:T(4,128)S(1)}, u32[]{:S(2)}) copy-start(f32[4,16]{1,0:T(4,128)S(1)} %get-tuple-element.3168) | copy-start | bytes 772
  4.6 47.8 %copy-start.48 = (f32[4,16]{1,0:T(4,128)}, f32[4,16]{1,0:T(4,128)S(1)}, u32[]{:S(2)}) copy-start(f32[4,16]{1,0:T(4,128)S(1)} %get-tuple-element.3167) | copy-start | bytes 772
  44.7 17.9 %copy-start.140 = (s32[5]{0:T(128)S(1)}, s32[5]{0:T(128)}, u32[]{:S(2)}) copy-start(s32[5]{0:T(128)} %constant.5190) | copy-start | bytes 64
  65.8 29.1 %copy-start.35 = (f32[4,1,1,256]{3,0,2,1:T(4,128)}, f32[4,1,1,256]{3,0,2,1:T(4,128)S(1)}, u32[]{:S(2)}) copy-start(f32[4,1,1,256]{3,0,2,1:T(4,128)S(1)} %concatenate.901) | copy-start | bytes 12292
  69.1 27.2 %copy-start.37 = (f32[4,1,1,256]{3,0,2,1:T(4,128)}, f32[4,1,1,256]{3,0,2,1:T(4,128)S(1)}, u32[]{:S(2)}) copy-start(f32[4,1,1,256]{3,0,2,1:T(4,128)S(1)} %concatenate.904) | copy-start | bytes 12292
  108.7 21.6 %collective-permute-start = (f32[1,4,1664]{2,1,0:T(4,128)S(1)}, f32[1,4,1664]{2,1,0:T(4,128)S(1)}, u32[]{:S(2)}, u32[]{:S(2)}) collective-permute-start(f32[1,4,1664]{2,1,0:T(4,128)S(1)} %maximum_bitcast_fusion), channel_id=1, source_target_pairs={{1,0},{2,1},{3,2},{4,3},{5,4},{6,5},{7,6},{8,7},{9,8},{10,9},{11,1... | collective-permute-start | bytes 79880 | tf_op jit(solution)/shard_map/ppermute | solution.py:19
  114.9 15.4 %collective-permute-start.1 = (f32[1,4,1664]{2,1,0:T(4,128)S(1)}, f32[1,4,1664]{2,1,0:T(4,128)S(1)}, u32[]{:S(2)}, u32[]{:S(2)}) collective-permute-start(f32[1,4,1664]{2,1,0:T(4,128)S(1)} %maximum_bitcast_fusion.1), channel_id=1, source_target_pairs={{0,1},{1,2},{2,3},{3,4},{4,5},{5,6},{6,7},{7,8},{8,9},{9,10},{10,1... | collective-permute-start | bytes 79880 | tf_op jit(solution)/shard_map/ppermute | solution.py:18
  119.9 17.8 %copy-start.99 = (pred[4]{0:T(512)(128)(4,1)}, pred[4]{0:T(512)(128)(4,1)S(1)}, u32[]{:S(2)}) copy-start(pred[4]{0:T(512)(128)(4,1)S(1)} %get-tuple-element.3202) | copy-start | bytes 16
  119.9 18.5 %copy-start.97 = (pred[4]{0:T(512)(128)(4,1)}, pred[4]{0:T(512)(128)(4,1)S(1)}, u32[]{:S(2)}) copy-start(pred[4]{0:T(512)(128)(4,1)S(1)} %get-tuple-element.3201) | copy-start | bytes 16
  120.2 16.3 %copy-start.71 = (s32[1024]{0:T(1024)}, s32[1024]{0:T(1024)S(1)}, u32[]{:S(2)}) copy-start(s32[1024]{0:T(1024)S(1)} %pad_clamp_fusion.12) | copy-start | bytes 12292
  140.1 385.0 %copy-start.68 = (f32[4,19,1]{1,0,2:T(4,128)S(1)}, f32[4,19,1]{1,0,2:T(4,128)}, u32[]{:S(2)}) copy-start(f32[4,19,1]{1,0,2:T(4,128)} %constant.5204) | copy-start | bytes 916
  149.0 25.2 %copy-start.20 = (f32[4,1,6,256]{3,0,2,1:T(4,128)S(1)}, f32[4,1,6,256]{3,0,2,1:T(4,128)}, u32[]{:S(2)}) copy-start(f32[4,1,6,256]{3,0,2,1:T(4,128)} %get-tuple-element.3882) | copy-start | bytes 73732 | tf_op jit(solution)/shard_map/while
  149.0 39.0 %copy-start.18 = (f32[4,1,6,256]{3,0,2,1:T(4,128)S(1)}, f32[4,1,6,256]{3,0,2,1:T(4,128)}, u32[]{:S(2)}) copy-start(f32[4,1,6,256]{3,0,2,1:T(4,128)} %get-tuple-element.3888) | copy-start | bytes 73732 | tf_op jit(solution)/shard_map/while
  566.6 18.0 %copy-start.27 = (f32[4,1,16,16]{3,2,0,1:T(8,128)S(1)}, f32[4,1,16,16]{3,2,0,1:T(8,128)}, u32[]{:S(2)}) copy-start(f32[4,1,16,16]{3,2,0,1:T(8,128)} %get-tuple-element.3479) | copy-start | bytes 12292
  566.6 18.0 %copy-start.28 = (f32[4,1,16,16]{3,2,0,1:T(8,128)S(1)}, f32[4,1,16,16]{3,2,0,1:T(8,128)}, u32[]{:S(2)}) copy-start(f32[4,1,16,16]{3,2,0,1:T(8,128)} %get-tuple-element.3480) | copy-start | bytes 12292
  617.9 19.3 %copy-start.108 = (pred[4]{0:T(512)(128)(4,1)S(1)}, pred[4]{0:T(512)(128)(4,1)}, u32[]{:S(2)}) copy-start(pred[4]{0:T(512)(128)(4,1)} %copy-done.107) | copy-start | bytes 16
  617.9 22.0 %copy-start.130 = (pred[4]{0:T(512)(128)(4,1)S(1)}, pred[4]{0:T(512)(128)(4,1)}, u32[]{:S(2)}) copy-start(pred[4]{0:T(512)(128)(4,1)} %copy-done.129) | copy-start | bytes 16
  617.9 22.1 %copy-start.128 = (pred[4]{0:T(512)(128)(4,1)S(1)}, pred[4]{0:T(512)(128)(4,1)}, u32[]{:S(2)}) copy-start(pred[4]{0:T(512)(128)(4,1)} %copy-done.127) | copy-start | bytes 16
  617.9 22.2 %copy-start.106 = (pred[4]{0:T(512)(128)(4,1)S(1)}, pred[4]{0:T(512)(128)(4,1)}, u32[]{:S(2)}) copy-start(pred[4]{0:T(512)(128)(4,1)} %copy-done.105) | copy-start | bytes 16
  617.9 22.9 %copy-start.104 = (pred[4]{0:T(512)(128)(4,1)S(1)}, pred[4]{0:T(512)(128)(4,1)}, u32[]{:S(2)}) copy-start(pred[4]{0:T(512)(128)(4,1)} %copy-done.103) | copy-start | bytes 16
  617.9 23.6 %copy-start.102 = (pred[4]{0:T(512)(128)(4,1)S(1)}, pred[4]{0:T(512)(128)(4,1)}, u32[]{:S(2)}) copy-start(pred[4]{0:T(512)(128)(4,1)} %copy-done.101) | copy-start | bytes 16
  617.9 24.2 %copy-start.126 = (pred[4]{0:T(512)(128)(4,1)S(1)}, pred[4]{0:T(512)(128)(4,1)}, u32[]{:S(2)}) copy-start(pred[4]{0:T(512)(128)(4,1)} %copy-done.125) | copy-start | bytes 16
  628.7 15.9 %collective-permute-start.2 = (f32[1,4,1664]{2,1,0:T(4,128)S(1)}, f32[1,4,1664]{2,1,0:T(4,128)S(1)}, u32[]{:S(2)}, u32[]{:S(2)}) collective-permute-start(f32[1,4,1664]{2,1,0:T(4,128)S(1)} %maximum_bitcast_fusion.2), channel_id=1, source_target_pairs={{1,0},{2,1},{3,2},{4,3},{5,4},{6,5},{7,6},{8,7},{9,8},{10,9},{11,1... | collective-permute-start | bytes 79880 | tf_op jit(solution)/shard_map/ppermute | solution.py:19
  634.6 10.0 collective-permute-start.3
  664.2 25.2 %copy-start.21 = (f32[4,1,6,256]{3,0,2,1:T(4,128)S(1)}, f32[4,1,6,256]{3,0,2,1:T(4,128)}, u32[]{:S(2)}) copy-start(f32[4,1,6,256]{3,0,2,1:T(4,128)} %get-tuple-element.3979) | copy-start | bytes 73732 | tf_op jit(solution)/shard_map/while
  664.2 39.0 %copy-start.19 = (f32[4,1,6,256]{3,0,2,1:T(4,128)S(1)}, f32[4,1,6,256]{3,0,2,1:T(4,128)}, u32[]{:S(2)}) copy-start(f32[4,1,6,256]{3,0,2,1:T(4,128)} %get-tuple-element.3985) | copy-start | bytes 73732 | tf_op jit(solution)/shard_map/while
  (115 other events, 845.7 us)
where the time goes:
time: 1050 us; the launch traced here: 1040 us
  local copies, waits for them, and re-layouts  929 us (88%)
  other arithmetic  67.3 us (6%)
  starting transfers between devices  14.6 us (1%)
  matrix products  12 us (1%)
  loops' own time  10.6 us (1%)
    scatter x60, local copies, waits for them, and re-layouts, propagate(): padded.at[(slice(None), lane_two) + spatial].set(face_values[:, member_num])  429 us
    scatter x12, local copies, waits for them, and re-layouts, propagate(): open_mask = open_mask.at[(slice(None),) + spatial].set(face_values[:, 5])  72.5 us
    scatter x24, local copies, waits for them, and re-layouts, propagate(): padded.at[(slice(None), opposite[lane_num]) + spatial]  61.5 us
    squeeze x6, local copies, waits for them, and re-layouts, make_slabs(): lax.index_in_dim(blocked, layer_index, axis_num + 2, keepdims=False)  41.3 us
    another operation x40, local copies, waits for them, and re-layouts, propagate(): jnp.stack(arrived_list, 1).reshape(block_count, 19, BLOCK * BLOCK * BLOCK)  39.5 us
    select_n x8, other arithmetic, propagate(): jnp.where(open_here > 0, pulled, blocked[:, opposite[lane_num]])  39.1 us
    another operation x68, local copies, waits for them, and re-layouts  33.8 us
    scatter x24, local copies, waits for them, and re-layouts, propagate(): open_mask.at[(slice(None),) + spatial].set(rim_edges[:, edge_num, 1])  31.7 us
  transfers between devices with their start and end apart: 4, of which 0 were waited for; matrix products, arithmetic and copies ran while one was open for 2% of the time, Pallas kernels for 0%

commit v1 on v0

v1 whole, which is shorter than its diff:
```python
import functools

import jax
import jax.numpy as jnp
import numpy as np
from jax import lax
from jax.experimental import pallas as pl
from jax.experimental.pallas import tpu as pltpu
from jax.sharding import PartitionSpec as P

SLOTS = 4
CELLS = 4096
LANES = 128
MESH = pl.DeviceIdType.MESH
CLOSED = np.float32(np.inf)


def velocities():
    found = [(0, 0, 0)]
    for axis in range(3):
        for sign in (1, -1):
            v = [0, 0, 0]
            v[axis] = sign
            found.append(tuple(v))
    for one, two in ((0, 1), (0, 2), (1, 2)):
        for sign_one in (1, -1):
            for sign_two in (1, -1):
                v = [0, 0, 0]
                v[one] = sign_one
                v[two] = sign_two
                found.append(tuple(v))
    return found


VEL = velocities()
OPP = [VEL.index(tuple(-c for c in v)) for v in VEL]
UP = [i for i, v in enumerate(VEL) if v[2] == 1]
DOWN = [i for i, v in enumerate(VEL) if v[2] == -1]

def column(direction):
    return VEL.index(direction) - 1


def collide(g, rate):
    sx, dx = g[1] + g[2], g[1] - g[2]
    sy, dy = g[3] + g[4], g[3] - g[4]
    sz, dz = g[5] + g[6], g[5] - g[6]

    def plane(first):
        a, b = g[first] + g[first + 3], g[first + 1] + g[first + 2]
        c, d = g[first] - g[first + 3], g[first + 1] - g[first + 2]
        return a + b, a - b, c + d, c - d

    exy, qxy, x1, y1 = plane(7)
    exz, qxz, x2, z1 = plane(11)
    eyz, qyz, y2, z2 = plane(15)
    sixth = np.float32(1 / 6)
    ux = (dx + 0.5 * (x1 + x2)) * sixth
    uy = (dy + 0.5 * (y1 + y2)) * sixth
    uz = (dz + 0.5 * (z1 + z2)) * sixth
    xx = (sx + sx) + (exy + exz)
    yy = (sy + sy) + (exy + eyz)
    zz = (sz + sz) + (exz + eyz)
    total = xx + yy + zz
    edges = exy + exz + eyz
    density = g[0] * np.float32(1 / 3) + (total - edges) * np.float32(1 / 36)
    ux2, uy2, uz2 = ux * ux, uy * uy, uz * uz
    u2 = ux2 + uy2 + uz2
    keep = 1.0 - rate
    quarter = 0.25 * keep
    base = density - u2 * sixth
    face = base + (keep * np.float32(1 / 3)) * u2 - (quarter * np.float32(1 / 3)) * total
    half_less = 0.5 - keep
    out = [None] * 19
    out[0] = base
    for first, along, u, square in ((1, xx, ux, ux2), (3, yy, uy, uy2), (5, zz, uz, uz2)):
        even = face + quarter * along + half_less * square
        out[first], out[first + 1] = even + u, even - u
    hx, hy, hz = 0.5 * ux2, 0.5 * uy2, 0.5 * uz2
    for first, ua, ub, ha, hb, q in (
        (7, ux, uy, hx, hy, qxy),
        (11, ux, uz, hx, hz, qxz),
        (15, uy, uz, hy, hz, qyz),
    ):
        cross = rate * (ua * ub) + quarter * q
        even = base + (ha + hb)
        plus, minus = even + cross, even - cross
        add, sub = ua + ub, ua - ub
        out[first], out[first + 3] = plus + add, plus - add
        out[first + 1], out[first + 2] = minus + sub, minus - sub
    return out


def roll(v, shift):
    shift = shift % LANES
    return v if shift == 0 else pltpu.roll(v, shift, 1)


def kernel(
    n_dev,
    x_hbm,
    flags_hbm,
    near_hbm,
    rate_ref,
    out_ref,
    x_ref,
    flags_ref,
    near_ref,
    c1_ref,
    c2_ref,
    g1_ref,
    index_ref,
    present_ref,
    fsend,
    fland,
    send1,
    send2,
    land1,
    land2,
    rim_ref,
    rim_y_ref,
    in_sem,
    small_sem,
    fsend_sem,
    frecv_sem,
    send_sem,
    recv_sem,
):
    me = lax.axis_index("dev")
    above, below = lax.rem(me + 1, n_dev), lax.rem(me + n_dev - 1, n_dev)
    to = (above, below)

    barrier = pltpu.get_barrier_semaphore()
    for other in to:
        pl.semaphore_signal(barrier, inc=1, device_id={"dev": other}, device_id_type=MESH)

    def fetch(r):
        part = pl.ds(r * 4, 4)
        return pltpu.make_async_copy(x_hbm.at[:, part], x_ref.at[:, part], in_sem.at[r])

    fetch_flags = pltpu.make_async_copy(flags_hbm, flags_ref, small_sem.at[0])
    fetch_near = pltpu.make_async_copy(near_hbm, near_ref, small_sem.at[1])
    fetch_flags.start()
    fetch_near.start()
    for r in range(4):
        fetch(r).start()

    lane = lax.broadcasted_iota(jnp.int32, (8, LANES), 1)
    row = lax.broadcasted_iota(jnp.int32, (8, LANES), 0)
    z = lane & 15
    z_rim = {1: z == 0, -1: z == 15}
    y_rim = {1: lane >= 112, -1: lane < 16}
    half = row >> 2

    rate = jnp.full((8, LANES), rate_ref[0], jnp.float32)
    for s in range(1, SLOTS):
        rate = jnp.where((row & 3) == s, rate_ref[s], rate)

    fetch_flags.wait()

    def pack_flags(q, _):
        pair = [(flags_ref[2 * q + k] > 0).astype(jnp.float32) for k in range(2)]
        up = jnp.where(z == 7, roll(pair[0], -8), 0.0) + jnp.where(z == 15, pair[1], 0.0)
        down = jnp.where(z == 0, pair[0], 0.0) + jnp.where(z == 8, roll(pair[1], 8), 0.0)
        for k in (1, 2, 4):
            up = up + roll(up, -k)
            down = down + roll(down, k)
        fsend[0, q] = up
        fsend[1, q] = down
        return 0

    lax.fori_loop(0, 8, pack_flags, 0)

    def flag_copy(side):
        return pltpu.make_async_remote_copy(
            src_ref=fsend.at[side],
            dst_ref=fland.at[side],
            send_sem=fsend_sem.at[side],
            recv_sem=frecv_sem.at[side],
            device_id={"dev": to[side]},
            device_id_type=MESH,
        )

    def value_copy(step, side, r):
        part = pl.ds(r * 2, 2)
        return pltpu.make_async_remote_copy(
            src_ref=(send1, send2)[step].at[side, part],
            dst_ref=(land1, land2)[step].at[side, part],
            send_sem=send_sem.at[step, side, r],
            recv_sem=recv_sem.at[step, side, r],
            device_id={"dev": to[side]},
            device_id_type=MESH,
        )

    fetch_near.wait()
    near = near_ref[...]
    near = jnp.concatenate([near, near], axis=0)
    entry = {d: jnp.broadcast_to(near[:, k : k + 1], (8, LANES)) for k, d in enumerate(VEL[1:])}
    for k, d in enumerate(VEL[1:]):
        slot, there = entry[d] & 3, entry[d] >= 0
        if d[1] == 0:
            index = slot + 4 * half
        else:
            own_half = half == (1 if d[1] == -1 else 0)
            main = (d[0], 0, d[2])
            if main == (0, 0, 0):
                slot = jnp.where(own_half, row & 3, slot)
                there = own_half | there
            else:
                slot = jnp.where(own_half, entry[main] & 3, slot)
                there = (own_half & (entry[main] >= 0)) | (jnp.logical_not(own_half) & there)
            index = slot + 4 * (1 - half)
        index_ref[k] = index
        present_ref[k] = there.astype(jnp.int32)

    def look(v, d):
        k = column(d)
        found = jnp.take_along_axis(v, index_ref[k], axis=0, mode="promise_in_bounds")
        return jnp.where(present_ref[k] > 0, found, CLOSED)

    pl.semaphore_wait(barrier, 2)
    for side in range(2):
        flag_copy(side).start()

    def collide_store(c_ref, x, k, g, packed):
        out = collide(g, rate)
        fluid = flags_ref[x] > 0
        for i in range(19):
            c_ref[i, x + 1] = jnp.where(fluid, out[i], CLOSED)
        for side, (members, source) in enumerate(((UP, 15), (DOWN, 0))):
            for p, i in enumerate(members):
                moved = roll(out[i], 8 * k + p - source)
                if packed[side] is None:
                    packed[side] = moved
                else:
                    packed[side] = jnp.where(z == 8 * k + p, moved, packed[side])

    def collide_all(step, c_ref, load):
        send = (send1, send2)[step]

        def part(r, _):
            if step == 0:
                fetch(r).wait()
            for qq in range(2):
                packed = [None, None]
                q = 2 * r + qq
                for k in range(2):
                    x = 2 * q + k
                    collide_store(c_ref, x, k, load(x, q, k), packed)
                for side in range(2):
                    send[side, q] = packed[side]
            for side in range(2):
                value_copy(step, side, r).start()
            return 0

        lax.fori_loop(0, 4, part, 0)

    def inner(c_ref, emit):
        for i in range(1, 19):
            cx, cy, cz = VEL[i]
            if cx:
                source, rim = (16, 0) if cx == 1 else (1, 17)
                c_ref[i, rim] = look(c_ref[i, source], (-cx, 0, 0))

        def settle(i, x, v):
            cx, cy, cz = VEL[i]
            v = roll(v, 16 * cy + cz)
            shut = v == CLOSED
            if cz:
                shut = shut | z_rim[cz]
            emit(i, x, jnp.where(shut, c_ref[OPP[i], x + 1], v))

        def part(r, _):
            for k in range(2):
                x = 2 * r + k
                emit(0, x, c_ref[0, x + 1])
                for i in range(1, 19):
                    cx, cy, cz = VEL[i]
                    v = c_ref[i, x + 1 - cx]
                    if cy:
                        v = jnp.where(y_rim[cy], look(v, (0, -cy, 0)), v)
                    settle(i, x, v)
            return 0

        lax.fori_loop(0, 8, part, 0)
        for i in range(1, 19):
            cx, cy, cz = VEL[i]
            if cx and cy:
                source, rim, x = (16, 0, 0) if cx == 1 else (1, 17, 15)
                v = jnp.where(y_rim[cy], look(c_ref[i, source], (-cx, -cy, 0)), c_ref[i, rim])
                settle(i, x, v)

    def arrive(step):
        land = (land1, land2)[step]
        for side in range(2):
            for r in range(4):
                value_copy(step, side, r).wait()
        for side, dz in ((0, -1), (1, 1)):
            for q in range(8):
                v = jnp.where(fland[side, q] > 0.0, land[side, q], CLOSED)
                face = look(v, (0, 0, dz))
                rim_ref[side, q + 1] = face
                for n, cy in enumerate((1, -1)):
                    rim_y_ref[side, n, q] = jnp.where(y_rim[cy], look(v, (0, -cy, dz)), face)
                if q == 7:
                    rim_ref[side, 0] = look(v, (-1, 0, dz))
                if q == 0:
                    rim_ref[side, 9] = look(v, (1, 0, dz))

    def outer(i, q, k, current):
        cx, cy, cz = VEL[i]
        side = 0 if cz == 1 else 1
        p = (UP if cz == 1 else DOWN).index(i)
        if cy:
            v, place = rim_y_ref[side, 0 if cy == 1 else 1, q], k
        else:
            v, place = rim_ref[side, q + 1 + (k - cx) // 2], (k - cx) % 2
        v = roll(v, (0 if cz == 1 else 15) - (8 * place + p) + 16 * cy)
        return jnp.where(z_rim[cz] & (v != CLOSED), v, current)

    collide_all(0, c1_ref, lambda x, q, k: [x_ref[i, x] for i in range(19)])

    def keep(i, x, v):
        g1_ref[i, x] = v

    inner(c1_ref, keep)
    for side in range(2):
        flag_copy(side).wait()
    arrive(0)

    def load_second(x, q, k):
        g = [g1_ref[i, x] for i in range(19)]
        return [outer(i, q, k, g[i]) if VEL[i][2] else g[i] for i in range(19)]

    collide_all(1, c2_ref, load_second)

    def finish(i, x, v):
        out_ref[i, x] = jnp.where(flags_ref[x] > 0, v, x_ref[i, x])

    def keep_or_finish(i, x, v):
        if VEL[i][2]:
            g1_ref[i, x] = v
        else:
            finish(i, x, v)

    inner(c2_ref, keep_or_finish)
    arrive(1)

    def last(q, _):
        for k in range(2):
            x = 2 * q + k
            for i in UP + DOWN:
                finish(i, x, outer(i, q, k, g1_ref[i, x]))
        return 0

    lax.fori_loop(0, 8, last, 0)


def body(populations, fluid_flags, neighbours, relax_rate):
    f32, i32 = jnp.float32, jnp.int32

    def vmem(*shape, kind=f32):
        return pltpu.VMEM(shape + (8, LANES), kind)

    tiles = populations.reshape(SLOTS, 19, 16, 2, LANES).transpose(1, 2, 3, 0, 4).reshape(19, 16, 8, LANES)
    flags = fluid_flags.reshape(SLOTS, 16, 2, LANES).transpose(1, 2, 0, 3).reshape(16, 8, LANES)
    done = pl.pallas_call(
        functools.partial(kernel, lax.axis_size("dev")),
        out_shape=jax.ShapeDtypeStruct((19, 16, 8, LANES), f32),
        in_specs=[
            pl.BlockSpec(memory_space=pltpu.HBM),
            pl.BlockSpec(memory_space=pltpu.HBM),
            pl.BlockSpec(memory_space=pltpu.HBM),
            pl.BlockSpec(memory_space=pltpu.SMEM),
        ],
        out_specs=pl.BlockSpec(memory_space=pltpu.VMEM),
        scratch_shapes=[
            vmem(19, 16),
            vmem(16, kind=i32),
            pltpu.VMEM((SLOTS, 18), i32),
            vmem(19, 18),
            vmem(19, 18),
            vmem(19, 16),
            vmem(18, kind=i32),
            vmem(18, kind=i32),
            vmem(2, 8),
            vmem(2, 8),
            vmem(2, 8),
            vmem(2, 8),
            vmem(2, 8),
            vmem(2, 8),
            vmem(2, 10),
            vmem(2, 2, 8),
            pltpu.SemaphoreType.DMA((4,)),
            pltpu.SemaphoreType.DMA((2,)),
            pltpu.SemaphoreType.DMA((2,)),
            pltpu.SemaphoreType.DMA((2,)),
            pltpu.SemaphoreType.DMA((2, 2, 4)),
            pltpu.SemaphoreType.DMA((2, 2, 4)),
        ],
        compiler_params=pltpu.CompilerParams(
            collective_id=0, has_side_effects=True, vmem_limit_bytes=40 * 2**20
        ),
        name="lattice_steps",
    )(tiles, flags, neighbours, relax_rate)
    back = done.reshape(19, 16, 2, SLOTS, LANES).transpose(3, 0, 1, 2, 4)
    return back.reshape(SLOTS, 19, CELLS)


def solution(mesh):
    placed = (
        P(("group", "dev"), None, None),
        P(("group", "dev"), None),
        P(("group", "dev"), None),
        P(("group", "dev")),
    )
    return jax.shard_map(
        body, mesh=mesh, in_specs=placed, out_specs=P(("group", "dev"), None, None), check_vma=False
    )
```

time: 1050 us -> 20.6 us (0.02)
  the two profiles are of different devices: /device:TPU:38 before, /device:TPU:0 now
where the time goes in v1:
time: 20.6 us; the launch traced here: 20.4 us
  Pallas kernels  15.9 us (77%)
  local copies, waits for them, and re-layouts  4.5 us (22%)
    pallas_call x1, Pallas kernels, body(): pl.pallas_call(functools.partial(kernel, lax.axis_size('dev')), out_shape...  15.9 us
    unnamed x9, local copies, waits for them, and re-layouts  4.5 us

profile of v1, /device:TPU:0, one launch (start us, length us, event | category | flops | bytes accessed | tf_op | source)
XLA Modules:
  0.0 20.4 jit_solution(17136346593534858131)
XLA Ops:
  0.0 0.0 copy-start
  0.0 1.3 %copy-done = f32[4,19,4096]{2,0,1:T(4,128)S(1)} copy-done((f32[4,19,4096]{2,0,1:T(4,128)S(1)}, f32[4,19,4096]{2,0,1:T(4,128)}, u32[]{:S(2)}) %copy-start) | copy-done | bytes 1245208
  1.3 0.0 copy-start.1
  1.3 0.8 %copy-done.1 = s32[4,4096]{1,0:T(4,128)S(1)} copy-done((s32[4,4096]{1,0:T(4,128)S(1)}, s32[4,4096]{1,0:T(4,128)}, u32[]{:S(2)}) %copy-start.1) | copy-done | bytes 65560
  2.1 0.0 copy-start.2
  2.1 0.7 %copy-done.2 = s32[4,18]{1,0:T(4,128)S(1)} copy-done((s32[4,18]{1,0:T(4,128)S(1)}, s32[4,18]{1,0:T(4,128)}, u32[]{:S(2)}) %copy-start.2) | copy-done | bytes 312
  2.8 0.0 copy-start.3
  2.8 0.7 %copy-done.3 = f32[4]{0:T(128)S(1)} copy-done((f32[4]{0:T(128)S(1)}, f32[4]{0:T(128)}, u32[]{:S(2)}) %copy-start.3) | copy-done | bytes 40
  3.5 15.9 %lattice_steps.1 = f32[19,16,8,128]{3,2,1,0:T(8,128)S(1)} custom-call(f32[19,16,8,128]{3,2,1,0:T(8,128)S(1)} %bitcast.16, s32[16,8,128]{2,1,0:T(8,128)S(1)} %bitcast.17, s32[4,18]{1,0:T(4,128)S(1)} %copy-done.2, f32[4]{0:T(128)S(1)} %copy-done.3), custom_call_target="tpu_custom_call" | custom-call | tf_op jit(solution)/shard_map/lattice_steps/pallas_call | solution.py:367
  19.4 1.0 %copy.9 = f32[4,19,4096]{2,0,1:T(4,128)} copy(f32[4,19,4096]{2,0,1:T(4,128)S(1)} %bitcast.15) | data formatting | bytes 2490368
Async XLA Ops:
  0.0 1.3 %copy-start = (f32[4,19,4096]{2,0,1:T(4,128)S(1)}, f32[4,19,4096]{2,0,1:T(4,128)}, u32[]{:S(2)}) copy-start(f32[4,19,4096]{2,0,1:T(4,128)} %param.4) | copy-start | bytes 3735556
  1.3 0.8 %copy-start.1 = (s32[4,4096]{1,0:T(4,128)S(1)}, s32[4,4096]{1,0:T(4,128)}, u32[]{:S(2)}) copy-start(s32[4,4096]{1,0:T(4,128)} %param.5) | copy-start | bytes 196612
  2.1 0.7 %copy-start.2 = (s32[4,18]{1,0:T(4,128)S(1)}, s32[4,18]{1,0:T(4,128)}, u32[]{:S(2)}) copy-start(s32[4,18]{1,0:T(4,128)} %near_hbm.1) | copy-start | bytes 868
  2.8 0.7 %copy-start.3 = (f32[4]{0:T(128)S(1)}, f32[4]{0:T(128)}, u32[]{:S(2)}) copy-start(f32[4]{0:T(128)} %rate_ref.1) | copy-start | bytes 52

commit v2 on v1

--- a/solution.py
+++ b/solution.py
@@ -127,12 +127,16 @@
     recv_sem,
 ):
     me = lax.axis_index("dev")
-    above, below = lax.rem(me + 1, n_dev), lax.rem(me + n_dev - 1, n_dev)
-    to = (above, below)
+    to = (lax.min(me + 1, n_dev - 1), lax.max(me - 1, 0))
+    sends = (me < n_dev - 1, me > 0)
+    hears = (me > 0, me < n_dev - 1)
 
     barrier = pltpu.get_barrier_semaphore()
-    for other in to:
-        pl.semaphore_signal(barrier, inc=1, device_id={"dev": other}, device_id_type=MESH)
+    for side in range(2):
+
+        @pl.when(sends[side])
+        def _(side=side):
+            pl.semaphore_signal(barrier, inc=1, device_id={"dev": to[side]}, device_id_type=MESH)
 
     def fetch(r):
         part = pl.ds(r * 4, 4)
@@ -158,7 +162,7 @@
 
     fetch_flags.wait()
 
-    def pack_flags(q, _):
+    for q in range(8):
         pair = [(flags_ref[2 * q + k] > 0).astype(jnp.float32) for k in range(2)]
         up = jnp.where(z == 7, roll(pair[0], -8), 0.0) + jnp.where(z == 15, pair[1], 0.0)
         down = jnp.where(z == 0, pair[0], 0.0) + jnp.where(z == 8, roll(pair[1], 8), 0.0)
@@ -167,9 +171,6 @@
             down = down + roll(down, k)
         fsend[0, q] = up
         fsend[1, q] = down
-        return 0
-
-    lax.fori_loop(0, 8, pack_flags, 0)
 
     def flag_copy(side):
         return pltpu.make_async_remote_copy(
@@ -218,9 +219,24 @@
         found = jnp.take_along_axis(v, index_ref[k], axis=0, mode="promise_in_bounds")
         return jnp.where(present_ref[k] > 0, found, CLOSED)
 
-    pl.semaphore_wait(barrier, 2)
+    def start(copy, side):
+        @pl.when(sends[side])
+        def _():
+            copy.start()
+
+    def sent(copy, side):
+        @pl.when(sends[side])
+        def _():
+            copy.wait_send()
+
+    def landed(copy, side):
+        @pl.when(hears[side])
+        def _():
+            copy.wait_recv()
+
+    pl.semaphore_wait(barrier, jnp.where(hears[0] & hears[1], 2, 1))
     for side in range(2):
-        flag_copy(side).start()
+        start(flag_copy(side), side)
 
     def collide_store(c_ref, x, k, g, packed):
         out = collide(g, rate)
@@ -250,7 +266,7 @@
                 for side in range(2):
                     send[side, q] = packed[side]
             for side in range(2):
-                value_copy(step, side, r).start()
+                start(value_copy(step, side, r), side)
             return 0
 
         lax.fori_loop(0, 4, part, 0)
@@ -294,7 +310,7 @@
         land = (land1, land2)[step]
         for side in range(2):
             for r in range(4):
-                value_copy(step, side, r).wait()
+                landed(value_copy(step, side, r), side)
         for side, dz in ((0, -1), (1, 1)):
             for q in range(8):
                 v = jnp.where(fland[side, q] > 0.0, land[side, q], CLOSED)
@@ -325,7 +341,7 @@
 
     inner(c1_ref, keep)
     for side in range(2):
-        flag_copy(side).wait()
+        landed(flag_copy(side), side)
     arrive(0)
 
     def load_second(x, q, k):
@@ -354,6 +370,11 @@
         return 0
 
     lax.fori_loop(0, 8, last, 0)
+    for side in range(2):
+        sent(flag_copy(side), side)
+        for step in range(2):
+            for r in range(4):
+                sent(value_copy(step, side, r), side)
 
 
 def body(populations, fluid_flags, neighbours, relax_rate):
@@ -399,7 +420,7 @@
             pltpu.SemaphoreType.DMA((2, 2, 4)),
         ],
         compiler_params=pltpu.CompilerParams(
-            collective_id=0, has_side_effects=True, vmem_limit_bytes=40 * 2**20
+            collective_id=0, has_side_effects=True, vmem_limit_bytes=62 * 2**20
         ),
         name="lattice_steps",
     )(tiles, flags, neighbours, relax_rate)

time: 20.6 us -> 16.5 us (0.80)
  the two profiles are of different devices: /device:TPU:0 before, /device:TPU:38 now
where the time goes in v2:
time: 16.5 us; the launch traced here: 16.3 us
  Pallas kernels  13.9 us (84%)
  local copies, waits for them, and re-layouts  2.44 us (15%)
    pallas_call x1, Pallas kernels, body(): pl.pallas_call(functools.partial(kernel, lax.axis_size('dev')), out_shape...  13.9 us
    unnamed x1, local copies, waits for them, and re-layouts  2.44 us

profile of v2, /device:TPU:38, one launch (start us, length us, event | category | flops | bytes accessed | tf_op | source)
XLA Modules:
  0.0 16.3 jit_solution(14211472868646985269)
XLA Ops:
  0.0 13.9 %lattice_steps.1 = f32[19,16,8,128]{3,2,1,0:T(8,128)} custom-call(f32[19,16,8,128]{3,2,1,0:T(8,128)} %bitcast.16, s32[16,8,128]{2,1,0:T(8,128)} %bitcast.17, s32[4,18]{1,0:T(4,128)} %near_hbm.1, f32[4]{0:T(128)} %rate_ref.1), custom_call_target="tpu_custom_call" | custom-call | tf_op jit(solution)/shard_map/lattice_steps/pallas_call | solution.py:388
  13.9 2.4 %copy.9 = f32[4,19,4096]{2,0,1:T(4,128)} copy(f32[4,19,4096]{2,0,1:T(4,128)} %bitcast.15) | data formatting | bytes 2490368

commit v3 on v1

v3 whole, which is shorter than its diff:
```python
import functools

import jax
import jax.numpy as jnp
import numpy as np
from jax import lax
from jax.experimental import pallas as pl
from jax.experimental.pallas import tpu as pltpu
from jax.sharding import PartitionSpec as P

SLOTS = 4
CELLS = 4096
LANES = 128
INNER = 4
MESH = pl.DeviceIdType.MESH
CLOSED = np.float32(np.inf)


def velocities():
    found = [(0, 0, 0)]
    for axis in range(3):
        for sign in (1, -1):
            v = [0, 0, 0]
            v[axis] = sign
            found.append(tuple(v))
    for one, two in ((0, 1), (0, 2), (1, 2)):
        for sign_one in (1, -1):
            for sign_two in (1, -1):
                v = [0, 0, 0]
                v[one] = sign_one
                v[two] = sign_two
                found.append(tuple(v))
    return found


VEL = velocities()
OPP = [VEL.index(tuple(-c for c in v)) for v in VEL]
UP = [i for i, v in enumerate(VEL) if v[2] == 1]
DOWN = [i for i, v in enumerate(VEL) if v[2] == -1]

def column(direction):
    return VEL.index(direction) - 1


def collide(g, rate):
    sx, dx = g[1] + g[2], g[1] - g[2]
    sy, dy = g[3] + g[4], g[3] - g[4]
    sz, dz = g[5] + g[6], g[5] - g[6]

    def plane(first):
        a, b = g[first] + g[first + 3], g[first + 1] + g[first + 2]
        c, d = g[first] - g[first + 3], g[first + 1] - g[first + 2]
        return a + b, a - b, c + d, c - d

    exy, qxy, x1, y1 = plane(7)
    exz, qxz, x2, z1 = plane(11)
    eyz, qyz, y2, z2 = plane(15)
    sixth = np.float32(1 / 6)
    ux = (dx + 0.5 * (x1 + x2)) * sixth
    uy = (dy + 0.5 * (y1 + y2)) * sixth
    uz = (dz + 0.5 * (z1 + z2)) * sixth
    xx = (sx + sx) + (exy + exz)
    yy = (sy + sy) + (exy + eyz)
    zz = (sz + sz) + (exz + eyz)
    total = xx + yy + zz
    edges = exy + exz + eyz
    density = g[0] * np.float32(1 / 3) + (total - edges) * np.float32(1 / 36)
    ux2, uy2, uz2 = ux * ux, uy * uy, uz * uz
    u2 = ux2 + uy2 + uz2
    keep = 1.0 - rate
    quarter = 0.25 * keep
    base = density - u2 * sixth
    face = base + (keep * np.float32(1 / 3)) * u2 - (quarter * np.float32(1 / 3)) * total
    half_less = 0.5 - keep
    out = [None] * 19
    out[0] = base
    for first, along, u, square in ((1, xx, ux, ux2), (3, yy, uy, uy2), (5, zz, uz, uz2)):
        even = face + quarter * along + half_less * square
        out[first], out[first + 1] = even + u, even - u
    hx, hy, hz = 0.5 * ux2, 0.5 * uy2, 0.5 * uz2
    for first, ua, ub, ha, hb, q in (
        (7, ux, uy, hx, hy, qxy),
        (11, ux, uz, hx, hz, qxz),
        (15, uy, uz, hy, hz, qyz),
    ):
        cross = rate * (ua * ub) + quarter * q
        even = base + (ha + hb)
        plus, minus = even + cross, even - cross
        add, sub = ua + ub, ua - ub
        out[first], out[first + 3] = plus + add, plus - add
        out[first + 1], out[first + 2] = minus + sub, minus - sub
    return out


def roll(v, shift):
    shift = shift % LANES
    return v if shift == 0 else pltpu.roll(v, shift, 1)


def turn(v, shift):
    return roll(v, shift) if isinstance(shift, int) else pltpu.roll(v, shift & (LANES - 1), 1)


def kernel(
    n_dev,
    x_hbm,
    flags_hbm,
    near_hbm,
    rate_ref,
    out_ref,
    x_ref,
    flags_ref,
    near_ref,
    c1_ref,
    c2_ref,
    g1_ref,
    index_ref,
    absent_ref,
    layer_ref,
    halo_ref,
    fsend,
    fland,
    send1,
    send2,
    land1,
    land2,
    in_sem,
    small_sem,
    fsend_sem,
    frecv_sem,
    send_sem,
    recv_sem,
):
    me = lax.axis_index("dev")
    to = (lax.min(me + 1, n_dev - 1), lax.max(me - 1, 0))
    sends = (me < n_dev - 1, me > 0)
    hears = (me > 0, me < n_dev - 1)

    def fetch(r):
        part = pl.ds(r * 4, 4)
        return pltpu.make_async_copy(x_hbm.at[:, part], x_ref.at[:, part], in_sem.at[r])

    fetch_flags = pltpu.make_async_copy(flags_hbm, flags_ref, small_sem.at[0])
    fetch_near = pltpu.make_async_copy(near_hbm, near_ref, small_sem.at[1])
    fetch_flags.start()
    fetch_near.start()
    for r in range(4):
        fetch(r).start()

    barrier = pltpu.get_barrier_semaphore()
    for side in range(2):

        @pl.when(sends[side])
        def _(side=side):
            pl.semaphore_signal(barrier, inc=1, device_id={"dev": to[side]}, device_id_type=MESH)

    lane = lax.broadcasted_iota(jnp.int32, (8, LANES), 1)
    row = lax.broadcasted_iota(jnp.int32, (8, LANES), 0)
    z = lane & 15
    z_rim = {1: z == 0, -1: z == 15}
    y_rim = {1: lane >= 112, -1: lane < 16}
    half = row >> 2

    rate = jnp.full((8, LANES), rate_ref[0], jnp.float32)
    for s in range(1, SLOTS):
        rate = jnp.where((row & 3) == s, rate_ref[s], rate)

    fetch_near.wait()
    near = near_ref[...]
    near = jnp.concatenate([near, near], axis=0)
    entry = {d: jnp.broadcast_to(near[:, k : k + 1], (8, LANES)) for k, d in enumerate(VEL[1:])}
    for k, d in enumerate(VEL[1:]):
        slot, there = entry[d] & 3, entry[d] >= 0
        if d[1] == 0:
            index = slot + 4 * half
        else:
            own_half = half == (1 if d[1] == -1 else 0)
            main = (d[0], 0, d[2])
            if main == (0, 0, 0):
                slot = jnp.where(own_half, row & 3, slot)
                there = own_half | there
            else:
                slot = jnp.where(own_half, entry[main] & 3, slot)
                there = (own_half & (entry[main] >= 0)) | (jnp.logical_not(own_half) & there)
            index = slot + 4 * (1 - half)
        index_ref[k] = index
        absent_ref[k] = jnp.where(there, 0.0, CLOSED)

    def look(v, d):
        k = column(d)
        return jnp.take_along_axis(v, index_ref[k], axis=0, mode="promise_in_bounds") + absent_ref[k]

    def gathered(x, v, layer, into):
        moved = turn(v, x - layer)
        return moved if into is None else jnp.where(z == x, moved, into)

    fetch_flags.wait()
    wet = [None, None]
    for x in range(16):
        flag = (flags_ref[x] > 0).astype(jnp.float32)
        for side, layer in enumerate((15, 0)):
            wet[side] = gathered(x, flag, layer, wet[side])
    for side in range(2):
        fsend[side] = wet[side]

    def flag_copy(side):
        return pltpu.make_async_remote_copy(
            src_ref=fsend.at[side],
            dst_ref=fland.at[side],
            send_sem=fsend_sem.at[side],
            recv_sem=frecv_sem.at[side],
            device_id={"dev": to[side]},
            device_id_type=MESH,
        )

    def value_copy(step, side):
        return pltpu.make_async_remote_copy(
            src_ref=(send1, send2)[step].at[side],
            dst_ref=(land1, land2)[step].at[side],
            send_sem=send_sem.at[step, side],
            recv_sem=recv_sem.at[step, side],
            device_id={"dev": to[side]},
            device_id_type=MESH,
        )

    def first(r, packed):
        fetch(r).wait()
        packed = list(packed)
        for k in range(4):
            x = 4 * r + k
            out = collide([x_ref[i, x] for i in range(19)], rate)
            fluid = flags_ref[x] > 0
            for i in range(19):
                c1_ref[i, x + 1] = jnp.where(fluid, out[i], CLOSED)
            for n, i in enumerate(UP + DOWN):
                packed[n] = gathered(x, out[i], 15 if n < 5 else 0, packed[n])
        return tuple(packed)

    packed = lax.fori_loop(0, 4, first, (jnp.zeros((8, LANES), jnp.float32),) * 10)
    for n in range(10):
        send1[n // 5, n % 5] = packed[n]

    pl.semaphore_wait(barrier, jnp.where(hears[0] & hears[1], 2, 1))
    for side in range(2):

        @pl.when(sends[side])
        def _(side=side):
            value_copy(0, side).start()
            flag_copy(side).start()

    def inner(c_ref, emit):
        for i in range(1, 19):
            cx, cy, cz = VEL[i]
            if cx:
                source, rim = (16, 0) if cx == 1 else (1, 17)
                c_ref[i, rim] = look(c_ref[i, source], (-cx, 0, 0))

        def settle(i, x, v):
            cx, cy, cz = VEL[i]
            v = roll(v, 16 * cy + cz)
            shut = v == CLOSED
            if cz:
                shut = shut | z_rim[cz]
            emit(i, x, jnp.where(shut, c_ref[OPP[i], x + 1], v))

        def part(r, _):
            for k in range(INNER):
                x = INNER * r + k
                emit(0, x, c_ref[0, x + 1])
                for i in range(1, 19):
                    cx, cy, cz = VEL[i]
                    v = c_ref[i, x + 1 - cx]
                    if cy:
                        v = jnp.where(y_rim[cy], look(v, (0, -cy, 0)), v)
                    settle(i, x, v)
            return 0

        lax.fori_loop(0, 16 // INNER, part, 0)
        for i in range(1, 19):
            cx, cy, cz = VEL[i]
            if cx and cy:
                source, rim, x = (16, 0, 0) if cx == 1 else (1, 17, 15)
                v = jnp.where(y_rim[cy], look(c_ref[i, source], (-cx, -cy, 0)), c_ref[i, rim])
                settle(i, x, v)

    def arrive(step, side):
        land = (land1, land2)[step]

        @pl.when(hears[side])
        def _():
            if step == 0:
                flag_copy(side).wait_recv()
            value_copy(step, side).wait_recv()

        halo = []
        for p, i in enumerate((UP, DOWN)[side]):
            cx, cy, cz = VEL[i]
            v = jnp.where(fland[side] > 0.0, land[side, p], CLOSED)
            face = look(v, (0, 0, -cz))
            if cx:
                away = roll(look(v, (-cx, 0, -cz)), -15 * cx)
                v = jnp.where(z == (0 if cx == 1 else 15), away, roll(face, cx))
            elif cy:
                v = roll(jnp.where(y_rim[cy], look(v, (0, -cy, -cz)), face), 16 * cy)
            else:
                v = face
            halo.append(v)
            halo_ref[step, side, p] = v
        return halo

    def outer(step, i, x, current):
        cz = VEL[i][2]
        side = 0 if cz == 1 else 1
        v = turn(halo_ref[step, side, (UP, DOWN)[side].index(i)], (0 if cz == 1 else 15) - x)
        return jnp.where(z_rim[cz] & (v != CLOSED), v, current)

    def keep(i, x, v):
        g1_ref[i, x] = v

    inner(c1_ref, keep)

    def gather_layers(i, _):
        low, high = None, None
        for x in range(16):
            v = g1_ref[i, x]
            low, high = gathered(x, v, 0, low), gathered(x, v, 15, high)
        layer_ref[0, i] = low
        layer_ref[1, i] = high
        return 0

    lax.fori_loop(0, 19, gather_layers, 0)

    for side in range(2):
        halo = arrive(0, side)
        g = [layer_ref[side, i] for i in range(19)]
        for i, v in zip((UP, DOWN)[side], halo):
            g[i] = jnp.where(v != CLOSED, v, g[i])
        out = collide(g, rate)
        for p, i in enumerate((DOWN, UP)[side]):
            send2[1 - side, p] = out[i]

        @pl.when(sends[1 - side])
        def _(side=side):
            value_copy(1, 1 - side).start()

    def second(r, _):
        for k in range(4):
            x = 4 * r + k
            g = [g1_ref[i, x] for i in range(19)]
            out = collide([outer(0, i, x, g[i]) if VEL[i][2] else g[i] for i in range(19)], rate)
            fluid = flags_ref[x] > 0
            for i in range(19):
                c2_ref[i, x + 1] = jnp.where(fluid, out[i], CLOSED)
        return 0

    lax.fori_loop(0, 4, second, 0)

    def finish(i, x, v):
        out_ref[i, x] = jnp.where(flags_ref[x] > 0, v, x_ref[i, x])

    def keep_or_finish(i, x, v):
        if VEL[i][2]:
            g1_ref[i, x] = v
        else:
            finish(i, x, v)

    inner(c2_ref, keep_or_finish)
    for side in range(2):
        arrive(1, side)

    def last(r, _):
        for k in range(4):
            x = 4 * r + k
            for i in UP + DOWN:
                finish(i, x, outer(1, i, x, g1_ref[i, x]))
        return 0

    lax.fori_loop(0, 4, last, 0)
    for side in range(2):

        @pl.when(sends[side])
        def _(side=side):
            flag_copy(side).wait_send()
            value_copy(0, side).wait_send()
            value_copy(1, side).wait_send()


def body(populations, fluid_flags, neighbours, relax_rate):
    f32, i32 = jnp.float32, jnp.int32

    def vmem(*shape, kind=f32):
        return pltpu.VMEM(shape + (8, LANES), kind)

    tiles = populations.reshape(SLOTS, 19, 16, 2, LANES).transpose(1, 2, 3, 0, 4).reshape(19, 16, 8, LANES)
    flags = fluid_flags.reshape(SLOTS, 16, 2, LANES).transpose(1, 2, 0, 3).reshape(16, 8, LANES)
    done = pl.pallas_call(
        functools.partial(kernel, lax.axis_size("dev")),
        out_shape=pltpu.VMEM((19, 16, 8, LANES), f32),
        in_specs=[
            pl.BlockSpec(memory_space=pltpu.HBM),
            pl.BlockSpec(memory_space=pltpu.HBM),
            pl.BlockSpec(memory_space=pltpu.HBM),
            pl.BlockSpec(memory_space=pltpu.SMEM),
        ],
        out_specs=pl.BlockSpec(memory_space=pltpu.VMEM),
        scratch_shapes=[
            vmem(19, 16),
            vmem(16, kind=i32),
            pltpu.VMEM((SLOTS, 18), i32),
            vmem(19, 18),
            vmem(19, 18),
            vmem(19, 16),
            vmem(18, kind=i32),
            vmem(18),
            vmem(2, 19),
            vmem(2, 2, 5),
            vmem(2),
            vmem(2),
            vmem(2, 5),
            vmem(2, 5),
            vmem(2, 5),
            vmem(2, 5),
            pltpu.SemaphoreType.DMA((4,)),
            pltpu.SemaphoreType.DMA((2,)),
            pltpu.SemaphoreType.DMA((2,)),
            pltpu.SemaphoreType.DMA((2,)),
            pltpu.SemaphoreType.DMA((2, 2)),
            pltpu.SemaphoreType.DMA((2, 2)),
        ],
        compiler_params=pltpu.CompilerParams(
            collective_id=0, has_side_effects=True, vmem_limit_bytes=62 * 2**20
        ),
        name="lattice_steps",
    )(tiles, flags, neighbours, relax_rate)
    back = done.reshape(19, 16, 2, SLOTS, LANES).transpose(3, 0, 1, 2, 4)
    return back.reshape(SLOTS, 19, CELLS)


def solution(mesh):
    placed = (
        P(("group", "dev"), None, None),
        P(("group", "dev"), None),
        P(("group", "dev"), None),
        P(("group", "dev")),
    )
    return jax.shard_map(
        body, mesh=mesh, in_specs=placed, out_specs=P(("group", "dev"), None, None), check_vma=False
    )
```

time: 20.6 us -> 12.3 us (0.60)
  the two profiles are of different devices: /device:TPU:0 before, /device:TPU:38 now
where the time goes in v3:
time: 12.3 us; the launch traced here: 12.1 us
  Pallas kernels  11.1 us (90%)
  local copies, waits for them, and re-layouts  1.04 us (8%)
    pallas_call x1, Pallas kernels, body(): pl.pallas_call(functools.partial(kernel, lax.axis_size('dev')), out_shape...  11.1 us
    unnamed x1, local copies, waits for them, and re-layouts  1.04 us

profile of v3, /device:TPU:38, one launch (start us, length us, event | category | flops | bytes accessed | tf_op | source)
XLA Modules:
  0.0 12.1 jit_solution(8949382288588931022)
XLA Ops:
  0.0 11.1 %lattice_steps.1 = f32[19,16,8,128]{3,2,1,0:T(8,128)S(1)} custom-call(f32[19,16,8,128]{3,2,1,0:T(8,128)} %bitcast.16, s32[16,8,128]{2,1,0:T(8,128)} %bitcast.17, s32[4,18]{1,0:T(4,128)} %near_hbm.1, f32[4]{0:T(128)} %rate_ref.1), custom_call_target="tpu_custom_call" | custom-call | tf_op jit(solution)/shard_map/lattice_steps/pallas_call | solution.py:396
  11.1 1.0 %copy.9 = f32[4,19,4096]{2,0,1:T(4,128)} copy(f32[4,19,4096]{2,0,1:T(4,128)S(1)} %bitcast.15) | data formatting | bytes 2490368

commit v4 on v3

--- a/solution.py
+++ b/solution.py
@@ -37,6 +37,9 @@
 OPP = [VEL.index(tuple(-c for c in v)) for v in VEL]
 UP = [i for i, v in enumerate(VEL) if v[2] == 1]
 DOWN = [i for i, v in enumerate(VEL) if v[2] == -1]
+
+PLANE = [i for i, v in enumerate(VEL) if v[2] == 0]
+
 
 def column(direction):
     return VEL.index(direction) - 1
@@ -116,18 +119,13 @@
     g1_ref,
     index_ref,
     absent_ref,
-    layer_ref,
     halo_ref,
-    fsend,
-    fland,
     send1,
     send2,
     land1,
     land2,
     in_sem,
     small_sem,
-    fsend_sem,
-    frecv_sem,
     send_sem,
     recv_sem,
 ):
@@ -169,26 +167,41 @@
     near = near_ref[...]
     near = jnp.concatenate([near, near], axis=0)
     entry = {d: jnp.broadcast_to(near[:, k : k + 1], (8, LANES)) for k, d in enumerate(VEL[1:])}
-    for k, d in enumerate(VEL[1:]):
-        slot, there = entry[d] & 3, entry[d] >= 0
-        if d[1] == 0:
-            index = slot + 4 * half
-        else:
-            own_half = half == (1 if d[1] == -1 else 0)
-            main = (d[0], 0, d[2])
-            if main == (0, 0, 0):
-                slot = jnp.where(own_half, row & 3, slot)
-                there = own_half | there
+    own = {d: (e & 3, e >= 0) for d, e in entry.items()}
+    theirs = {}
+    for d in VEL[1:]:
+        if d[2]:
+            e = entry[tuple(-c for c in d)]
+            slot, there = row & 3, None
+            for m in range(4):
+                named = pltpu.roll(e, m, 0) if m else e
+                match = named == (1 - d[2]) * 4 + (row & 3)
+                slot = jnp.where(match, (row - m) & 3, slot)
+                there = match if there is None else there | match
+            theirs[d] = (slot, there)
+
+    for table, first_row in ((own, 0), (theirs, 18)):
+        for d, (slot, there) in table.items():
+            if d[1] == 0:
+                index = slot + 4 * half
             else:
-                slot = jnp.where(own_half, entry[main] & 3, slot)
-                there = (own_half & (entry[main] >= 0)) | (jnp.logical_not(own_half) & there)
-            index = slot + 4 * (1 - half)
-        index_ref[k] = index
-        absent_ref[k] = jnp.where(there, 0.0, CLOSED)
+                own_half = half == (1 if d[1] == -1 else 0)
+                main = (d[0], 0, d[2])
+                main_slot, main_there = (row & 3, row >= 0) if main == (0, 0, 0) else table[main]
+                slot = jnp.where(own_half, main_slot, slot)
+                there = (own_half & main_there) | (jnp.logical_not(own_half) & there)
+                index = slot + 4 * (1 - half)
+            index_ref[first_row + column(d)] = index
+            absent_ref[first_row + column(d)] = jnp.where(there, 0.0, CLOSED)
 
     def look(v, d):
         k = column(d)
         return jnp.take_along_axis(v, index_ref[k], axis=0, mode="promise_in_bounds") + absent_ref[k]
+
+    def look_across(v, d, first_row=0):
+        k = first_row + column(d)
+        found = jnp.take_along_axis(v, index_ref[k], axis=0, mode="promise_in_bounds")
+        return jnp.where(absent_ref[k] > 0.0, CLOSED, found)
 
     def gathered(x, v, layer, into):
         moved = turn(v, x - layer)
@@ -201,17 +214,8 @@
         for side, layer in enumerate((15, 0)):
             wet[side] = gathered(x, flag, layer, wet[side])
     for side in range(2):
-        fsend[side] = wet[side]
-
-    def flag_copy(side):
-        return pltpu.make_async_remote_copy(
-            src_ref=fsend.at[side],
-            dst_ref=fland.at[side],
-            send_sem=fsend_sem.at[side],
-            recv_sem=frecv_sem.at[side],
-            device_id={"dev": to[side]},
-            device_id_type=MESH,
-        )
+        send1[side, 5] = wet[side]
+        send2[side, 14] = rate
 
     def value_copy(step, side):
         return pltpu.make_async_remote_copy(
@@ -246,7 +250,6 @@
         @pl.when(sends[side])
         def _(side=side):
             value_copy(0, side).start()
-            flag_copy(side).start()
 
     def inner(c_ref, emit):
         for i in range(1, 19):
@@ -283,30 +286,20 @@
                 v = jnp.where(y_rim[cy], look(c_ref[i, source], (-cx, -cy, 0)), c_ref[i, rim])
                 settle(i, x, v)
 
-    def arrive(step, side):
-        land = (land1, land2)[step]
-
+    def landed(step, side):
         @pl.when(hears[side])
         def _():
-            if step == 0:
-                flag_copy(side).wait_recv()
             value_copy(step, side).wait_recv()
 
-        halo = []
-        for p, i in enumerate((UP, DOWN)[side]):
-            cx, cy, cz = VEL[i]
-            v = jnp.where(fland[side] > 0.0, land[side, p], CLOSED)
-            face = look(v, (0, 0, -cz))
-            if cx:
-                away = roll(look(v, (-cx, 0, -cz)), -15 * cx)
-                v = jnp.where(z == (0 if cx == 1 else 15), away, roll(face, cx))
-            elif cy:
-                v = roll(jnp.where(y_rim[cy], look(v, (0, -cy, -cz)), face), 16 * cy)
-            else:
-                v = face
-            halo.append(v)
-            halo_ref[step, side, p] = v
-        return halo
+    def crossed(v, i, first_row=0):
+        cx, cy, cz = VEL[i]
+        face = look_across(v, (0, 0, -cz), first_row)
+        if cx:
+            away = roll(look_across(v, (-cx, 0, -cz), first_row), -15 * cx)
+            return jnp.where(z == (0 if cx == 1 else 15), away, roll(face, cx))
+        if cy:
+            return roll(jnp.where(y_rim[cy], look_across(v, (0, -cy, -cz), first_row), face), 16 * cy)
+        return face
 
     def outer(step, i, x, current):
         cz = VEL[i][2]
@@ -319,29 +312,22 @@
 
     inner(c1_ref, keep)
 
-    def gather_layers(i, _):
-        low, high = None, None
-        for x in range(16):
-            v = g1_ref[i, x]
-            low, high = gathered(x, v, 0, low), gathered(x, v, 15, high)
-        layer_ref[0, i] = low
-        layer_ref[1, i] = high
-        return 0
-
-    lax.fori_loop(0, 19, gather_layers, 0)
-
-    for side in range(2):
-        halo = arrive(0, side)
-        g = [layer_ref[side, i] for i in range(19)]
-        for i, v in zip((UP, DOWN)[side], halo):
-            g[i] = jnp.where(v != CLOSED, v, g[i])
-        out = collide(g, rate)
-        for p, i in enumerate((DOWN, UP)[side]):
-            send2[1 - side, p] = out[i]
-
-        @pl.when(sends[1 - side])
+    for side, layer in enumerate((15, 0)):
+        for n, i in enumerate(PLANE + (UP, DOWN)[side]):
+            into = None
+            for x in range(16):
+                into = gathered(x, g1_ref[i, x], layer, into)
+            send2[side, n] = into
+
+        @pl.when(sends[side])
         def _(side=side):
-            value_copy(1, 1 - side).start()
+            value_copy(1, side).start()
+
+    for side in range(2):
+        landed(0, side)
+        for p, i in enumerate((UP, DOWN)[side]):
+            v = jnp.where(land1[side, 5] > 0.0, land1[side, p], CLOSED)
+            halo_ref[0, side, p] = crossed(v, i)
 
     def second(r, _):
         for k in range(4):
@@ -366,7 +352,18 @@
 
     inner(c2_ref, keep_or_finish)
     for side in range(2):
-        arrive(1, side)
+        theirs_out, theirs_in = (UP, DOWN) if side == 0 else (DOWN, UP)
+        landed(1, side)
+        g = [None] * 19
+        for n, i in enumerate(PLANE + theirs_out):
+            g[i] = land2[side, n]
+        for p, i in enumerate(theirs_in):
+            v = jnp.where(send1[1 - side, 5] > 0.0, send1[1 - side, p], CLOSED)
+            v = crossed(v, i, 18)
+            g[i] = jnp.where(v != CLOSED, v, land1[side, theirs_out.index(OPP[i])])
+        out = collide(g, land2[side, 14])
+        for p, i in enumerate(theirs_out):
+            halo_ref[1, side, p] = crossed(jnp.where(land1[side, 5] > 0.0, out[i], CLOSED), i)
 
     def last(r, _):
         for k in range(4):
@@ -380,7 +377,6 @@
 
         @pl.when(sends[side])
         def _(side=side):
-            flag_copy(side).wait_send()
             value_copy(0, side).wait_send()
             value_copy(1, side).wait_send()
 
@@ -410,19 +406,14 @@
             vmem(19, 18),
             vmem(19, 18),
             vmem(19, 16),
-            vmem(18, kind=i32),
-            vmem(18),
-            vmem(2, 19),
+            vmem(36, kind=i32),
+            vmem(36),
             vmem(2, 2, 5),
-            vmem(2),
-            vmem(2),
-            vmem(2, 5),
-            vmem(2, 5),
-            vmem(2, 5),
-            vmem(2, 5),
+            vmem(2, 6),
+            vmem(2, 15),
+            vmem(2, 6),
+            vmem(2, 15),
             pltpu.SemaphoreType.DMA((4,)),
-            pltpu.SemaphoreType.DMA((2,)),
-            pltpu.SemaphoreType.DMA((2,)),
             pltpu.SemaphoreType.DMA((2,)),
             pltpu.SemaphoreType.DMA((2, 2)),
             pltpu.SemaphoreType.DMA((2, 2)),

time: 12.3 us -> 10.4 us (0.85)
  Pallas kernels: 11.1 us -> 9.25 us
    pallas_call x1, Pallas kernels: 11.1 us -> 9.25 us  [body(): pl.pallas_call(functools.partial(kernel, lax.axis_size('dev')), out_shape...]
where the time goes in v4:
time: 10.4 us; the launch traced here: 10.3 us
  Pallas kernels  9.25 us (89%)
  local copies, waits for them, and re-layouts  1.04 us (10%)
    pallas_call x1, Pallas kernels, body(): pl.pallas_call(functools.partial(kernel, lax.axis_size('dev')), out_shape...  9.25 us
    unnamed x1, local copies, waits for them, and re-layouts  1.04 us

profile of v4, /device:TPU:38, one launch (start us, length us, event | category | flops | bytes accessed | tf_op | source)
XLA Modules:
  0.0 10.3 jit_solution(11974540604044786561)
XLA Ops:
  0.0 9.2 %lattice_steps.1 = f32[19,16,8,128]{3,2,1,0:T(8,128)S(1)} custom-call(f32[19,16,8,128]{3,2,1,0:T(8,128)} %bitcast.16, s32[16,8,128]{2,1,0:T(8,128)} %bitcast.17, s32[4,18]{1,0:T(4,128)} %near_hbm.1, f32[4]{0:T(128)} %rate_ref.1), custom_call_target="tpu_custom_call" | custom-call | tf_op jit(solution)/shard_map/lattice_steps/pallas_call | solution.py:392
  9.3 1.0 %copy.9 = f32[4,19,4096]{2,0,1:T(4,128)} copy(f32[4,19,4096]{2,0,1:T(4,128)S(1)} %bitcast.15) | data formatting | bytes 2490368

commit v5 on v4

--- a/solution.py
+++ b/solution.py
@@ -100,6 +100,63 @@
     return v if shift == 0 else pltpu.roll(v, shift, 1)
 
 
+def weighted(terms):
+    groups = {}
+    for factor, v in terms:
+        if factor:
+            groups.setdefault(abs(factor), []).append((factor > 0, v))
+    total = None
+    for factor, members in sorted(groups.items()):
+        part = None
+        for positive, v in members:
+            if part is None:
+                part = v if positive else -v
+            else:
+                part = part + v if positive else part - v
+        part = part * np.float32(factor)
+        total = part if total is None else total + part
+    return total
+
+
+def crossing_moments(g):
+    weight = {i: (12, 2, 1)[sum(map(abs, VEL[i]))] / 36 for i in g}
+
+    def total(factor):
+        return weighted([(factor(*VEL[i], weight[i]), v) for i, v in g.items()])
+
+    return [
+        total(lambda x, y, z, w: w),
+        total(lambda x, y, z, w: 3 * x * w),
+        total(lambda x, y, z, w: 3 * y * w),
+        total(lambda x, y, z, w: 3 * z * w),
+        total(lambda x, y, z, w: x * z),
+        total(lambda x, y, z, w: y * z),
+        total(lambda x, y, z, w: 12 * w * (3 * z * z - x * x - y * y - z * z)),
+    ]
+
+
+def collide_crossing(moments, rate, members):
+    density, ux, uy, uz, qxz, qyz, zz = moments
+    sixth = np.float32(1 / 6)
+    keep = 1.0 - rate
+    quarter = 0.25 * keep
+    u2 = ux * ux + uy * uy + uz * uz
+    base = density - u2 * sixth
+    out = []
+    for i in members:
+        cx, cy, cz = VEL[i]
+        if cx or cy:
+            u, q, sign = (ux, qxz, cx) if cx else (uy, qyz, cy)
+            cross = rate * (u * uz) + quarter * q
+            even = base + 0.5 * (u * u + uz * uz)
+            even = even + cross if sign * cz > 0 else even - cross
+            even = even + u if sign > 0 else even - u
+        else:
+            even = base + (keep * np.float32(1 / 3)) * u2 + quarter * zz + (0.5 - keep) * (uz * uz)
+        out.append(even + uz if cz > 0 else even - uz)
+    return out
+
+
 def turn(v, shift):
     return roll(v, shift) if isinstance(shift, int) else pltpu.roll(v, shift & (LANES - 1), 1)
 
@@ -215,15 +272,15 @@
             wet[side] = gathered(x, flag, layer, wet[side])
     for side in range(2):
         send1[side, 5] = wet[side]
-        send2[side, 14] = rate
-
-    def value_copy(step, side):
+        send1[side, 6] = rate
+
+    def value_copy(step, side, target=None):
         return pltpu.make_async_remote_copy(
             src_ref=(send1, send2)[step].at[side],
             dst_ref=(land1, land2)[step].at[side],
             send_sem=send_sem.at[step, side],
             recv_sem=recv_sem.at[step, side],
-            device_id={"dev": to[side]},
+            device_id={"dev": to[side] if target is None else target},
             device_id_type=MESH,
         )
 
@@ -244,14 +301,18 @@
     for n in range(10):
         send1[n // 5, n % 5] = packed[n]
 
-    pl.semaphore_wait(barrier, jnp.where(hears[0] & hears[1], 2, 1))
-    for side in range(2):
-
-        @pl.when(sends[side])
-        def _(side=side):
-            value_copy(0, side).start()
-
-    def inner(c_ref, emit):
+    second_core = (me & 1) == 1
+
+    def send_first():
+        pl.semaphore_wait(barrier, jnp.where(hears[0] & hears[1], 2, 1))
+        early = jnp.where(second_core, 0, 1)
+        for side in (early, 1 - early):
+
+            @pl.when(((side == 0) & sends[0]) | ((side == 1) & sends[1]))
+            def _(side=side):
+                value_copy(0, side, jnp.where(side == 0, to[0], to[1])).start()
+
+    def inner(c_ref, emit, between=None):
         for i in range(1, 19):
             cx, cy, cz = VEL[i]
             if cx:
@@ -278,7 +339,13 @@
                     settle(i, x, v)
             return 0
 
-        lax.fori_loop(0, 16 // INNER, part, 0)
+        steps = 16 // INNER
+        if between is None:
+            lax.fori_loop(0, steps, part, 0)
+        else:
+            lax.fori_loop(0, steps // 2, part, 0)
+            between()
+            lax.fori_loop(steps // 2, steps, part, 0)
         for i in range(1, 19):
             cx, cy, cz = VEL[i]
             if cx and cy:
@@ -310,18 +377,31 @@
     def keep(i, x, v):
         g1_ref[i, x] = v
 
-    inner(c1_ref, keep)
-
-    for side, layer in enumerate((15, 0)):
-        for n, i in enumerate(PLANE + (UP, DOWN)[side]):
+    inner(c1_ref, keep, send_first)
+
+    def send_second(side):
+        g = {}
+        for i in PLANE + (UP, DOWN)[side]:
             into = None
             for x in range(16):
-                into = gathered(x, g1_ref[i, x], layer, into)
-            send2[side, n] = into
+                into = gathered(x, g1_ref[i, x], (15, 0)[side], into)
+            g[i] = into
+        for n, v in enumerate(crossing_moments(g)):
+            send2[side, n] = v
 
         @pl.when(sends[side])
-        def _(side=side):
+        def _():
             value_copy(1, side).start()
+
+    @pl.when(second_core)
+    def _():
+        send_second(0)
+
+    send_second(1)
+
+    @pl.when(jnp.logical_not(second_core))
+    def _():
+        send_second(0)
 
     for side in range(2):
         landed(0, side)
@@ -354,16 +434,15 @@
     for side in range(2):
         theirs_out, theirs_in = (UP, DOWN) if side == 0 else (DOWN, UP)
         landed(1, side)
-        g = [None] * 19
-        for n, i in enumerate(PLANE + theirs_out):
-            g[i] = land2[side, n]
+        g = {}
         for p, i in enumerate(theirs_in):
             v = jnp.where(send1[1 - side, 5] > 0.0, send1[1 - side, p], CLOSED)
             v = crossed(v, i, 18)
             g[i] = jnp.where(v != CLOSED, v, land1[side, theirs_out.index(OPP[i])])
-        out = collide(g, land2[side, 14])
+        moments = [land2[side, n] + v for n, v in enumerate(crossing_moments(g))]
+        out = collide_crossing(moments, land1[side, 6], theirs_out)
         for p, i in enumerate(theirs_out):
-            halo_ref[1, side, p] = crossed(jnp.where(land1[side, 5] > 0.0, out[i], CLOSED), i)
+            halo_ref[1, side, p] = crossed(jnp.where(land1[side, 5] > 0.0, out[p], CLOSED), i)
 
     def last(r, _):
         for k in range(4):
@@ -409,10 +488,10 @@
             vmem(36, kind=i32),
             vmem(36),
             vmem(2, 2, 5),
-            vmem(2, 6),
-            vmem(2, 15),
-            vmem(2, 6),
-            vmem(2, 15),
+            vmem(2, 7),
+            vmem(2, 7),
+            vmem(2, 7),
+            vmem(2, 7),
             pltpu.SemaphoreType.DMA((4,)),
             pltpu.SemaphoreType.DMA((2,)),
             pltpu.SemaphoreType.DMA((2, 2)),

time: 10.4 us -> 10.8 us (1.038)
  Pallas kernels: 9.25 us -> 9.58 us
    pallas_call x1, Pallas kernels: 9.25 us -> 9.58 us  [body(): pl.pallas_call(functools.partial(kernel, lax.axis_size('dev')), out_shape...]
where the time goes in v5:
time: 10.8 us; the launch traced here: 10.6 us
  Pallas kernels  9.58 us (89%)
  local copies, waits for them, and re-layouts  1.04 us (10%)
    pallas_call x1, Pallas kernels, body(): pl.pallas_call(functools.partial(kernel, lax.axis_size('dev')), out_shape...  9.58 us
    unnamed x1, local copies, waits for them, and re-layouts  1.04 us

profile of v5, /device:TPU:38, one launch (start us, length us, event | category | flops | bytes accessed | tf_op | source)
XLA Modules:
  0.0 10.6 jit_solution(17527483061237648257)
XLA Ops:
  0.0 9.6 %lattice_steps.1 = f32[19,16,8,128]{3,2,1,0:T(8,128)S(1)} custom-call(f32[19,16,8,128]{3,2,1,0:T(8,128)} %bitcast.16, s32[16,8,128]{2,1,0:T(8,128)} %bitcast.17, s32[4,18]{1,0:T(4,128)} %near_hbm.1, f32[4]{0:T(128)} %rate_ref.1), custom_call_target="tpu_custom_call" | custom-call | tf_op jit(solution)/shard_map/lattice_steps/pallas_call | solution.py:471
  9.6 1.0 %copy.9 = f32[4,19,4096]{2,0,1:T(4,128)} copy(f32[4,19,4096]{2,0,1:T(4,128)S(1)} %bitcast.15) | data formatting | bytes 2490368

commit v6 on v5

--- a/solution.py
+++ b/solution.py
@@ -168,6 +168,7 @@
     near_hbm,
     rate_ref,
     out_ref,
+    late_ref,
     x_ref,
     flags_ref,
     near_ref,
@@ -312,7 +313,7 @@
             def _(side=side):
                 value_copy(0, side, jnp.where(side == 0, to[0], to[1])).start()
 
-    def inner(c_ref, emit, between=None):
+    def inner(c_ref, emit):
         for i in range(1, 19):
             cx, cy, cz = VEL[i]
             if cx:
@@ -339,13 +340,7 @@
                     settle(i, x, v)
             return 0
 
-        steps = 16 // INNER
-        if between is None:
-            lax.fori_loop(0, steps, part, 0)
-        else:
-            lax.fori_loop(0, steps // 2, part, 0)
-            between()
-            lax.fori_loop(steps // 2, steps, part, 0)
+        lax.fori_loop(0, 16 // INNER, part, 0)
         for i in range(1, 19):
             cx, cy, cz = VEL[i]
             if cx and cy:
@@ -368,16 +363,17 @@
             return roll(jnp.where(y_rim[cy], look_across(v, (0, -cy, -cz), first_row), face), 16 * cy)
         return face
 
-    def outer(step, i, x, current):
+    def outer(i, x, current):
         cz = VEL[i][2]
         side = 0 if cz == 1 else 1
-        v = turn(halo_ref[step, side, (UP, DOWN)[side].index(i)], (0 if cz == 1 else 15) - x)
+        v = turn(halo_ref[side, (UP, DOWN)[side].index(i)], (0 if cz == 1 else 15) - x)
         return jnp.where(z_rim[cz] & (v != CLOSED), v, current)
 
     def keep(i, x, v):
         g1_ref[i, x] = v
 
-    inner(c1_ref, keep, send_first)
+    send_first()
+    inner(c1_ref, keep)
 
     def send_second(side):
         g = {}
@@ -407,13 +403,13 @@
         landed(0, side)
         for p, i in enumerate((UP, DOWN)[side]):
             v = jnp.where(land1[side, 5] > 0.0, land1[side, p], CLOSED)
-            halo_ref[0, side, p] = crossed(v, i)
+            halo_ref[side, p] = crossed(v, i)
 
     def second(r, _):
         for k in range(4):
             x = 4 * r + k
             g = [g1_ref[i, x] for i in range(19)]
-            out = collide([outer(0, i, x, g[i]) if VEL[i][2] else g[i] for i in range(19)], rate)
+            out = collide([outer(i, x, g[i]) if VEL[i][2] else g[i] for i in range(19)], rate)
             fluid = flags_ref[x] > 0
             for i in range(19):
                 c2_ref[i, x + 1] = jnp.where(fluid, out[i], CLOSED)
@@ -424,13 +420,8 @@
     def finish(i, x, v):
         out_ref[i, x] = jnp.where(flags_ref[x] > 0, v, x_ref[i, x])
 
-    def keep_or_finish(i, x, v):
-        if VEL[i][2]:
-            g1_ref[i, x] = v
-        else:
-            finish(i, x, v)
-
-    inner(c2_ref, keep_or_finish)
+    inner(c2_ref, finish)
+
     for side in range(2):
         theirs_out, theirs_in = (UP, DOWN) if side == 0 else (DOWN, UP)
         landed(1, side)
@@ -442,16 +433,9 @@
         moments = [land2[side, n] + v for n, v in enumerate(crossing_moments(g))]
         out = collide_crossing(moments, land1[side, 6], theirs_out)
         for p, i in enumerate(theirs_out):
-            halo_ref[1, side, p] = crossed(jnp.where(land1[side, 5] > 0.0, out[p], CLOSED), i)
-
-    def last(r, _):
-        for k in range(4):
-            x = 4 * r + k
-            for i in UP + DOWN:
-                finish(i, x, outer(1, i, x, g1_ref[i, x]))
-        return 0
-
-    lax.fori_loop(0, 4, last, 0)
+            v = crossed(jnp.where(land1[side, 5] > 0.0, out[p], CLOSED), i)
+            late_ref[side, p] = jnp.where(send1[1 - side, 5] > 0.0, v, CLOSED)
+
     for side in range(2):
 
         @pl.when(sends[side])
@@ -460,6 +444,25 @@
             value_copy(1, side).wait_send()
 
 
+def finish_kernel(held_ref, late_ref, out_hbm, done_ref, sem):
+    def write(i):
+        source = done_ref.at[(UP + DOWN).index(i)] if VEL[i][2] else held_ref.at[i]
+        return pltpu.make_async_copy(source, out_hbm.at[i], sem.at[i])
+
+    for i in PLANE:
+        write(i).start()
+    z = lax.broadcasted_iota(jnp.int32, (8, LANES), 1) & 15
+    for n, i in enumerate(UP + DOWN):
+        rim = 0 if n < 5 else 15
+        late = late_ref[n // 5, n % 5]
+        for x in range(16):
+            v = roll(late, rim - x)
+            done_ref[n, x] = jnp.where((z == rim) & (v != CLOSED), v, held_ref[i, x])
+        write(i).start()
+    for i in range(19):
+        write(i).wait()
+
+
 def body(populations, fluid_flags, neighbours, relax_rate):
     f32, i32 = jnp.float32, jnp.int32
 
@@ -468,16 +471,16 @@
 
     tiles = populations.reshape(SLOTS, 19, 16, 2, LANES).transpose(1, 2, 3, 0, 4).reshape(19, 16, 8, LANES)
     flags = fluid_flags.reshape(SLOTS, 16, 2, LANES).transpose(1, 2, 0, 3).reshape(16, 8, LANES)
-    done = pl.pallas_call(
+    held, late = pl.pallas_call(
         functools.partial(kernel, lax.axis_size("dev")),
-        out_shape=pltpu.VMEM((19, 16, 8, LANES), f32),
+        out_shape=(pltpu.VMEM((19, 16, 8, LANES), f32), pltpu.VMEM((2, 5, 8, LANES), f32)),
         in_specs=[
             pl.BlockSpec(memory_space=pltpu.HBM),
             pl.BlockSpec(memory_space=pltpu.HBM),
             pl.BlockSpec(memory_space=pltpu.HBM),
             pl.BlockSpec(memory_space=pltpu.SMEM),
         ],
-        out_specs=pl.BlockSpec(memory_space=pltpu.VMEM),
+        out_specs=(pl.BlockSpec(memory_space=pltpu.VMEM),) * 2,
         scratch_shapes=[
             vmem(19, 16),
             vmem(16, kind=i32),
@@ -487,7 +490,7 @@
             vmem(19, 16),
             vmem(36, kind=i32),
             vmem(36),
-            vmem(2, 2, 5),
+            vmem(2, 5),
             vmem(2, 7),
             vmem(2, 7),
             vmem(2, 7),
@@ -502,6 +505,15 @@
         ),
         name="lattice_steps",
     )(tiles, flags, neighbours, relax_rate)
+    done = pl.pallas_call(
+        finish_kernel,
+        out_shape=jax.ShapeDtypeStruct((19, 16, 8, LANES), f32),
+        in_specs=[pl.BlockSpec(memory_space=pltpu.VMEM)] * 2,
+        out_specs=pl.BlockSpec(memory_space=pltpu.HBM),
+        scratch_shapes=[vmem(10, 16), pltpu.SemaphoreType.DMA((19,))],
+        compiler_params=pltpu.CompilerParams(vmem_limit_bytes=16 * 2**20),
+        name="finish",
+    )(held, late)
     back = done.reshape(19, 16, 2, SLOTS, LANES).transpose(3, 0, 1, 2, 4)
     return back.reshape(SLOTS, 19, CELLS)
 

time: 10.8 us -> 10.2 us (0.944)
  local copies, waits for them, and re-layouts: 1.04 us -> 0 us
  Pallas kernels: 9.58 us -> 10 us
    pallas_call x0 -> x1, Pallas kernels: none -> 1.18 us  [body(): pl.pallas_call(finish_kernel, out_shape=jax.ShapeDtypeStruct((19, 16, 8,...]
    unnamed x1 -> x0, local copies, waits for them, and re-layouts: 1.04 us -> none
    pallas_call x1, Pallas kernels: 9.58 us -> 8.86 us  [body(): pl.pallas_call(functools.partial(kernel, lax.axis_size('dev')), out_shape...]
where the time goes in v6:
time: 10.2 us; the launch traced here: 10 us
  Pallas kernels  10 us (98%)
    pallas_call x1, Pallas kernels, body(): pl.pallas_call(functools.partial(kernel, lax.axis_size('dev')), out_shape...  8.86 us
    pallas_call x1, Pallas kernels, body(): pl.pallas_call(finish_kernel, out_shape=jax.ShapeDtypeStruct((19, 16, 8,...  1.18 us

profile of v6, /device:TPU:38, one launch (start us, length us, event | category | flops | bytes accessed | tf_op | source)
XLA Modules:
  0.0 10.0 jit_solution(7881073014916042586)
XLA Ops:
  0.0 8.9 %lattice_steps.1 = (f32[19,16,8,128]{3,2,1,0:T(8,128)S(1)}, f32[2,5,8,128]{3,2,1,0:T(8,128)S(1)}) custom-call(f32[19,16,8,128]{3,2,1,0:T(8,128)} %bitcast.15, s32[16,8,128]{2,1,0:T(8,128)} %bitcast.16, s32[4,18]{1,0:T(4,128)} %near_hbm.1, f32[4]{0:T(128)} %rate_ref.1), custom_call_target="tpu_custom_call" | custom-call | tf_op jit(solution)/shard_map/lattice_steps/pallas_call | solution.py:474
  8.9 1.2 %finish.1 = f32[19,16,8,128]{3,2,1,0:T(8,128)} custom-call(f32[19,16,8,128]{3,2,1,0:T(8,128)S(1)} %get-tuple-element.7.held_ref, f32[2,5,8,128]{3,2,1,0:T(8,128)S(1)} %get-tuple-element.8.late_ref), custom_call_target="tpu_custom_call" | custom-call | tf_op jit(solution)/shard_map/finish/pallas_call | solution.py:508

commit v7 on v6

--- a/solution.py
+++ b/solution.py
@@ -177,7 +177,8 @@
     g1_ref,
     index_ref,
     absent_ref,
-    halo_ref,
+    layer_ref,
+    wet_ref,
     send1,
     send2,
     land1,
@@ -266,14 +267,15 @@
         return moved if into is None else jnp.where(z == x, moved, into)
 
     fetch_flags.wait()
-    wet = [None, None]
+    wet = [None] * 4
     for x in range(16):
         flag = (flags_ref[x] > 0).astype(jnp.float32)
-        for side, layer in enumerate((15, 0)):
+        for side, layer in enumerate((15, 0, 14, 1)):
             wet[side] = gathered(x, flag, layer, wet[side])
     for side in range(2):
         send1[side, 5] = wet[side]
         send1[side, 6] = rate
+        wet_ref[side] = wet[2 + side]
 
     def value_copy(step, side, target=None):
         return pltpu.make_async_remote_copy(
@@ -363,12 +365,6 @@
             return roll(jnp.where(y_rim[cy], look_across(v, (0, -cy, -cz), first_row), face), 16 * cy)
         return face
 
-    def outer(i, x, current):
-        cz = VEL[i][2]
-        side = 0 if cz == 1 else 1
-        v = turn(halo_ref[side, (UP, DOWN)[side].index(i)], (0 if cz == 1 else 15) - x)
-        return jnp.where(z_rim[cz] & (v != CLOSED), v, current)
-
     def keep(i, x, v):
         g1_ref[i, x] = v
 
@@ -382,6 +378,7 @@
             for x in range(16):
                 into = gathered(x, g1_ref[i, x], (15, 0)[side], into)
             g[i] = into
+            layer_ref[side, i] = into
         for n, v in enumerate(crossing_moments(g)):
             send2[side, n] = v
 
@@ -398,18 +395,12 @@
     @pl.when(jnp.logical_not(second_core))
     def _():
         send_second(0)
-
-    for side in range(2):
-        landed(0, side)
-        for p, i in enumerate((UP, DOWN)[side]):
-            v = jnp.where(land1[side, 5] > 0.0, land1[side, p], CLOSED)
-            halo_ref[side, p] = crossed(v, i)
 
     def second(r, _):
         for k in range(4):
             x = 4 * r + k
             g = [g1_ref[i, x] for i in range(19)]
-            out = collide([outer(i, x, g[i]) if VEL[i][2] else g[i] for i in range(19)], rate)
+            out = collide(g, rate)
             fluid = flags_ref[x] > 0
             for i in range(19):
                 c2_ref[i, x + 1] = jnp.where(fluid, out[i], CLOSED)
@@ -421,6 +412,38 @@
         out_ref[i, x] = jnp.where(flags_ref[x] > 0, v, x_ref[i, x])
 
     inner(c2_ref, finish)
+
+    def in_plane(v, i):
+        cx, cy, _ = VEL[i]
+        here = jnp.where(y_rim[cy], look_across(v, (0, -cy, 0)), v) if cy else v
+        here = roll(here, 16 * cy + cx)
+        if cx:
+            away = look_across(v, (-cx, 0, 0))
+            if cy:
+                away = jnp.where(y_rim[cy], look_across(v, (-cx, -cy, 0)), away)
+            here = jnp.where(z == (0 if cx == 1 else 15), roll(away, 16 * cy - 15 * cx), here)
+        return here
+
+    for side in range(2):
+        outs, ins = (UP, DOWN) if side == 0 else (DOWN, UP)
+        arriving = 1 - side
+        landed(0, arriving)
+        g = {i: layer_ref[side, i] for i in PLANE + outs}
+        for p, i in enumerate(ins):
+            v = crossed(jnp.where(land1[arriving, 5] > 0.0, land1[arriving, p], CLOSED), i)
+            g[i] = jnp.where(v != CLOSED, v, send1[side, outs.index(OPP[i])])
+        fluid, below_fluid = send1[side, 5] > 0.0, wet_ref[side] > 0.0
+        c = [jnp.where(fluid, v, CLOSED) for v in collide([g[i] for i in range(19)], rate)]
+        late_ref[side, 0] = c[0]
+        for i in PLANE[1:]:
+            v = in_plane(c[i], i)
+            late_ref[side, i] = jnp.where(fluid, jnp.where(v != CLOSED, v, c[OPP[i]]), CLOSED)
+        for i in outs:
+            v = in_plane(jnp.where(below_fluid, 0.0, CLOSED), i)
+            late_ref[side, i] = jnp.where(v == CLOSED, c[OPP[i]], CLOSED)
+        for p, i in enumerate(ins):
+            late_ref[side, i] = c[OPP[i]]
+            late_ref[side, 19 + p] = jnp.where(below_fluid, in_plane(c[i], i), CLOSED)
 
     for side in range(2):
         theirs_out, theirs_in = (UP, DOWN) if side == 0 else (DOWN, UP)
@@ -434,7 +457,7 @@
         out = collide_crossing(moments, land1[side, 6], theirs_out)
         for p, i in enumerate(theirs_out):
             v = crossed(jnp.where(land1[side, 5] > 0.0, out[p], CLOSED), i)
-            late_ref[side, p] = jnp.where(send1[1 - side, 5] > 0.0, v, CLOSED)
+            late_ref[1 - side, i] = jnp.where((send1[1 - side, 5] > 0.0) & (v != CLOSED), v, late_ref[1 - side, i])
 
     for side in range(2):
 
@@ -445,22 +468,24 @@
 
 
 def finish_kernel(held_ref, late_ref, out_hbm, done_ref, sem):
-    def write(i):
-        source = done_ref.at[(UP + DOWN).index(i)] if VEL[i][2] else held_ref.at[i]
-        return pltpu.make_async_copy(source, out_hbm.at[i], sem.at[i])
-
-    for i in PLANE:
-        write(i).start()
     z = lax.broadcasted_iota(jnp.int32, (8, LANES), 1) & 15
-    for n, i in enumerate(UP + DOWN):
-        rim = 0 if n < 5 else 15
-        late = late_ref[n // 5, n % 5]
+    copies = []
+    for i in range(19):
+        parts = [(15, late_ref[0, i]), (0, late_ref[1, i])]
+        if i in DOWN:
+            parts.append((14, late_ref[0, 19 + DOWN.index(i)]))
+        if i in UP:
+            parts.append((1, late_ref[1, 19 + UP.index(i)]))
         for x in range(16):
-            v = roll(late, rim - x)
-            done_ref[n, x] = jnp.where((z == rim) & (v != CLOSED), v, held_ref[i, x])
-        write(i).start()
-    for i in range(19):
-        write(i).wait()
+            v = held_ref[i, x]
+            for at, late in parts:
+                moved = roll(late, at - x)
+                v = jnp.where((z == at) & (moved != CLOSED), moved, v)
+            done_ref[i, x] = v
+        copies.append(pltpu.make_async_copy(done_ref.at[i], out_hbm.at[i], sem.at[i]))
+        copies[-1].start()
+    for copy in copies:
+        copy.wait()
 
 
 def body(populations, fluid_flags, neighbours, relax_rate):
@@ -473,7 +498,7 @@
     flags = fluid_flags.reshape(SLOTS, 16, 2, LANES).transpose(1, 2, 0, 3).reshape(16, 8, LANES)
     held, late = pl.pallas_call(
         functools.partial(kernel, lax.axis_size("dev")),
-        out_shape=(pltpu.VMEM((19, 16, 8, LANES), f32), pltpu.VMEM((2, 5, 8, LANES), f32)),
+        out_shape=(pltpu.VMEM((19, 16, 8, LANES), f32), pltpu.VMEM((2, 24, 8, LANES), f32)),
         in_specs=[
             pl.BlockSpec(memory_space=pltpu.HBM),
             pl.BlockSpec(memory_space=pltpu.HBM),
@@ -490,7 +515,8 @@
             vmem(19, 16),
             vmem(36, kind=i32),
             vmem(36),
-            vmem(2, 5),
+            vmem(2, 19),
+            vmem(2),
             vmem(2, 7),
             vmem(2, 7),
             vmem(2, 7),
@@ -510,7 +536,7 @@
         out_shape=jax.ShapeDtypeStruct((19, 16, 8, LANES), f32),
         in_specs=[pl.BlockSpec(memory_space=pltpu.VMEM)] * 2,
         out_specs=pl.BlockSpec(memory_space=pltpu.HBM),
-        scratch_shapes=[vmem(10, 16), pltpu.SemaphoreType.DMA((19,))],
+        scratch_shapes=[vmem(19, 16), pltpu.SemaphoreType.DMA((19,))],
         compiler_params=pltpu.CompilerParams(vmem_limit_bytes=16 * 2**20),
         name="finish",
     )(held, late)

time: 10.2 us -> 10 us (0.980)
  Pallas kernels: 10 us -> 9.87 us
    pallas_call x1, Pallas kernels: 8.86 us -> 8.24 us  [body(): pl.pallas_call(functools.partial(kernel, lax.axis_size('dev')), out_shape...]
    pallas_call x1, Pallas kernels: 1.18 us -> 1.63 us  [body(): pl.pallas_call(finish_kernel, out_shape=jax.ShapeDtypeStruct((19, 16, 8,...]
where the time goes in v7:
time: 10 us; the launch traced here: 9.88 us
  Pallas kernels  9.87 us (99%)
    pallas_call x1, Pallas kernels, body(): pl.pallas_call(functools.partial(kernel, lax.axis_size('dev')), out_shape...  8.24 us
    pallas_call x1, Pallas kernels, body(): pl.pallas_call(finish_kernel, out_shape=jax.ShapeDtypeStruct((19, 16, 8,...  1.63 us

profile of v7, /device:TPU:38, one launch (start us, length us, event | category | flops | bytes accessed | tf_op | source)
XLA Modules:
  0.0 9.9 jit_solution(5644121311441580660)
XLA Ops:
  0.0 8.2 %lattice_steps.1 = (f32[19,16,8,128]{3,2,1,0:T(8,128)S(1)}, f32[2,24,8,128]{3,2,1,0:T(8,128)S(1)}) custom-call(f32[19,16,8,128]{3,2,1,0:T(8,128)} %bitcast.15, s32[16,8,128]{2,1,0:T(8,128)} %bitcast.16, s32[4,18]{1,0:T(4,128)} %near_hbm.1, f32[4]{0:T(128)} %rate_ref.1), custom_call_target="tpu_custom_call" | custom-call | tf_op jit(solution)/shard_map/lattice_steps/pallas_call | solution.py:499
  8.3 1.6 %finish.1 = f32[19,16,8,128]{3,2,1,0:T(8,128)} custom-call(f32[19,16,8,128]{3,2,1,0:T(8,128)S(1)} %get-tuple-element.7.held_ref, f32[2,24,8,128]{3,2,1,0:T(8,128)S(1)} %get-tuple-element.8.late_ref), custom_call_target="tpu_custom_call" | custom-call | tf_op jit(solution)/shard_map/finish/pallas_call | solution.py:534
